TPU v7x, 512 devices: a whole 4x8x8 slice. The times are simulated.
512 devices in a mesh: patch: 64 (over y, x, core), band: 8 (over z).
Axes of the slice: x: 4, y: 8, z: 8, core: 2. Of those that a mesh axis runs over, the one named last changes fastest.
Arguments:
- nodes: bfloat16 [65536, 512], P(('patch', 'band')), may hold values from -6 to 6
- edges: bfloat16 [393216, 512], P(('patch', 'band')), may hold values from -6 to 6
- d_new_edges: bfloat16 [393216, 512], P(('patch', 'band')), may hold values from -6 to 6
- d_aggregate: bfloat16 [65536, 512], P(('patch', 'band')), may hold values from -6 to 6
- edge_w1: bfloat16 [1536, 512], replicated, may hold values from -0.15625 to 0.15625
- edge_w2: bfloat16 [512, 512], replicated, may hold values from -0.25 to 0.25
- senders: int32 [393216], P(('patch', 'band')), may hold values from 0 to 65535, as said below
- receivers: int32 [393216], P(('patch', 'band')), may hold values from 0 to 127
- edge_count: int32 [512], P(('patch', 'band')), may hold values from 307 to 768, as said below
Outputs:
- d_nodes: bfloat16 [65536, 512], P(('patch', 'band'))
- d_edges: bfloat16 [393216, 512], P(('patch', 'band'))
- d_edge_w1: float32 [1536, 512], P('patch')
Inputs may be any that keep to these rules, and one draw needn't show every extreme that they name: `senders`: each sender has the band of its edge slot's device and lies in that slot's device, among the last 32 nodes of the device one patch lower, or among the first 32 nodes of the device one patch higher (patches taken cyclically). `edge_count`: some device has all 768 slots live.
All inputs are finite; a program needn't handle non-finite values.
Results may differ from a plain program's by a relative error of at most 0.017.
Values may be sent and summed in bfloat16 or wider, within the bound.
No kernel may reach another device: no remote copies, remote signals or barrier semaphores. Data moves between devices by JAX's collectives and lax.ppermute only.
A program may use at most 64 MiB of HBM per device.

v0:
```python
import jax
import jax.numpy as jnp
from jax import lax
from jax.sharding import PartitionSpec as P

HALO = 32


def with_halo(array, sides, width):
    for axis, dim in sides:
        devices, length = (lax.axis_size(axis), array.shape[dim])
        up = [(i, (i + 1) % devices) for i in range(devices)]
        down = [(j, i) for i, j in up]
        last = lax.slice_in_dim(array, length - width, length, axis=dim)
        leading = lax.slice_in_dim(array, 0, width, axis=dim)
        before = lax.ppermute(last, axis, up)
        after = lax.ppermute(leading, axis, down)
        array = jnp.concatenate([before, array, after], axis=dim)
    return array


def shifted(block, axis, distance):
    devices = range(lax.axis_size(axis))
    route = [((i - distance) % len(devices), i) for i in devices]
    return lax.ppermute(block, axis, route)


def edge_grads(stacked, grad_new, edge_w1, edge_w2):
    pre = jnp.dot(stacked, edge_w1, preferred_element_type=jnp.float32)
    hidden = jax.nn.silu(pre).astype(jnp.bfloat16)
    out = jnp.dot(hidden, edge_w2, preferred_element_type=jnp.float32)
    center = out - jnp.mean(out, axis=-1, keepdims=True)
    rstd = lax.rsqrt(jnp.mean(center * center, axis=-1, keepdims=True) + 1e-05)
    normed = center * rstd
    g_out = (
        grad_new
        - jnp.mean(grad_new, axis=-1, keepdims=True)
        - normed * jnp.mean(grad_new * normed, axis=-1, keepdims=True)
    ) * rstd
    g_out = g_out.astype(jnp.bfloat16)
    g_hidden = lax.dot_general(
        g_out, edge_w2, (((1,), (1,)), ((), ())), preferred_element_type=jnp.float32
    )
    sigma = jax.nn.sigmoid(pre)
    dz = (g_hidden * sigma * (1.0 + pre * (1.0 - sigma))).astype(jnp.bfloat16)
    grad_in = lax.dot_general(
        dz, edge_w1, (((1,), (1,)), ((), ())), preferred_element_type=jnp.float32
    )
    return (dz, grad_in)


def one_hot_rows(index, count):
    return (index[:, None] == jnp.arange(count, dtype=jnp.int32)[None, :]).astype(jnp.bfloat16)


def collect(hot, values):
    return lax.dot_general(
        hot.astype(jnp.float32),
        values,
        (((0,), (0,)), ((), ())),
        preferred_element_type=jnp.float32,
        precision=lax.Precision.HIGHEST,
    )


def per_device(
    nodes, edges, d_new_edges, d_aggregate, edge_w1, edge_w2, senders, receivers, edge_count
):
    rows = nodes.shape[0]
    slots = edges.shape[0]
    width = nodes.shape[1]
    npatch = lax.axis_size("patch")
    nband = lax.axis_size("band")
    here = lax.axis_index("patch")
    lower = (here - 1) % npatch
    owner_patch = senders // rows // nband
    offset = senders % rows
    table = with_halo(nodes, (("patch", 0),), HALO)
    position = jnp.where(
        owner_patch == here,
        HALO + offset,
        jnp.where(owner_patch == lower, offset - (rows - HALO), HALO + rows + offset),
    )
    send_hot = one_hot_rows(position, table.shape[0])
    recv_hot = one_hot_rows(receivers, rows)
    sender_rows = jnp.dot(send_hot, table, preferred_element_type=jnp.float32).astype(jnp.bfloat16)
    receiver_rows = jnp.dot(recv_hot, nodes, preferred_element_type=jnp.float32).astype(
        jnp.bfloat16
    )
    aggregate_rows = jnp.dot(recv_hot, d_aggregate, preferred_element_type=jnp.float32)
    stacked = jnp.concatenate([edges, sender_rows, receiver_rows], axis=1)
    live = (jnp.arange(slots, dtype=jnp.int32) < edge_count[0]).astype(jnp.float32)[:, None]
    grad_new = live * (d_new_edges.astype(jnp.float32) + aggregate_rows)
    dz, grad_in = edge_grads(stacked, grad_new, edge_w1, edge_w2)
    table_grad = collect(send_hot, grad_in[:, width : 2 * width])
    own = table_grad[HALO : HALO + rows]
    below = table_grad[:HALO]
    above = table_grad[HALO + rows :]
    from_upper = shifted(below.astype(jnp.bfloat16), "patch", -1).astype(below.dtype)
    from_lower = shifted(above.astype(jnp.bfloat16), "patch", 1).astype(above.dtype)
    node_grad = own + collect(recv_hot, grad_in[:, 2 * width :])
    node_grad = node_grad.at[:HALO].add(from_lower)
    node_grad = node_grad.at[rows - HALO :].add(from_upper)
    local_weight = lax.dot_general(
        stacked, dz, (((0,), (0,)), ((), ())), preferred_element_type=jnp.float32
    )
    band_total_weight = lax.psum(local_weight.astype(jnp.bfloat16), "band").astype(jnp.float32)
    weight_grad = lax.psum_scatter(band_total_weight, "patch", scatter_dimension=0, tiled=True)
    edge_grad = (grad_new + grad_in[:, :width]).astype(jnp.bfloat16)
    return (node_grad.astype(jnp.bfloat16), edge_grad, weight_grad)


def solution(mesh):
    placed = (
        P(("patch", "band"), None),
        P(("patch", "band"), None),
        P(("patch", "band"), None),
        P(("patch", "band"), None),
        P(),
        P(),
        P(("patch", "band")),
        P(("patch", "band")),
        P(("patch", "band")),
    )
    return jax.shard_map(
        per_device,
        mesh=mesh,
        in_specs=placed,
        out_specs=(P(("patch", "band"), None), P(("patch", "band"), None), P("patch", None)),
        check_vma=False,
    )
```

profile of v0, /device:TPU:64, one launch (start us, length us, event | category | flops | bytes accessed | tf_op | source)
XLA Modules:
  0.0 280.5 jit_solution(8288989487973507918)
XLA Ops:
  7.2 0.0 copy-start
  7.2 0.0 copy-start.3
  7.2 0.0 copy-start.4
  7.2 0.0 all-reduce.3.cloned.1.call-start
  7.2 0.9 fusion.35
  8.2 1.9 collective-permute-start
  10.1 7.0 %collective-permute-start.1 = (bf16[32,512]{1,0:T(8,128)(2,1)S(1)}, bf16[32,512]{1,0:T(8,128)(2,1)S(1)}, u32[]{:S(2)}, u32[]{:S(2)}) collective-permute-start(bf16[32,512]{1,0:T(8,128)(2,1)S(1)} %get-tuple-element.38), channel_id=1, source_target_pairs={{8,0},{16,8},{24,16},{32,24},{40,32},{48,40},{56,48},{64,56},{72,6... | collective-permute-start | bytes 98312 | tf_op jit(solution)/shard_map/ppermute | solution.py:17
  17.8 2.3 convolution_convert_fusion.1
  20.1 0.7 select_select_fusion
  20.8 0.0 copy-done.3
  20.8 0.0 copy-start.7
  20.9 1.2 copy.17
  22.0 0.0 copy-done.4
  22.0 0.3 copy.16
  22.3 0.0 collective-permute-done
  22.3 0.0 collective-permute-done.1
  22.3 0.0 copy-done.7
  22.3 0.6 convolution_convert_fusion.2
  22.9 0.0 copy-done
  22.9 0.0 copy-start.10
  22.9 2.8 %fusion.7 = f32[768,512]{1,0:T(8,128)S(1)} fusion(bf16[1536,512]{1,0:T(8,128)(2,1)S(1)} %copy-done, bf16[768,512]{0,1:T(8,128)(2,1)} %convolution_convert_fusion.1, bf16[768,512]{0,1:T(8,128)(2,1)S(1)} %convolution_convert_fusion.2, bf16[768,512]{0,1:T(8,128)(2,1)} %copy.17), kind=kOutput, calls=%fused_computation.17 | convolution fusion | flops 1215037440 | bytes 5505024 | tf_op jit(solution)/shard_map/dot_general | solution.py:29
  25.7 0.0 copy-done.10
  25.8 0.7 fusion.36
  26.5 0.0 copy-start.8
  26.5 0.0 copy-start.9
  26.5 0.2 multiply_reduce_fusion.1
  26.7 0.7 copy-done.8
  27.4 0.0 copy-done.9
  27.4 0.7 fusion.33
  28.2 0.0 copy-start.1
  28.2 1.2 copy-done.1
  29.4 0.0 copy-start.5
  29.4 0.0 copy-start.6
  29.4 1.1 multiply_convert_fusion
  30.5 0.1 copy-done.5
  30.5 0.2 copy-done.6
  30.8 2.5 convolution_convert_fusion
  33.3 0.0 all-reduce.3.cloned.1.call-update
  33.3 0.0 reduce-scatter.4.cloned.1.call-start
  33.4 85.9 %all-reduce.3.cloned.1.call-done = bf16[1536,512]{1,0:T(8,128)(2,1)} async-done(((bf16[1536,512]{1,0:T(8,128)(2,1)}), bf16[1536,512]{1,0:T(8,128)(2,1)}) %all-reduce.3.cloned.1.call-update) | async-done | bytes 1572880 | tf_op jit(solution)/shard_map/psum | solution.py:107
  119.2 3.5 %convert_element_type.61 = f32[1536,512]{1,0:T(8,128)} convert(bf16[1536,512]{1,0:T(8,128)(2,1)} %all-reduce.3.cloned.1.call-done) | non-fusion elementwise | flops 786432 | bytes 4718592 | tf_op jit(solution)/shard_map/convert_element_type | solution.py:107
  122.7 0.0 reduce-scatter.4.cloned.1.call-update
  122.8 1.4 fusion.38
  124.2 0.0 copy-start.2
  124.2 0.1 slice.81
  124.3 2.0 copy-done.2
  126.3 1.1 fusion.37
  127.4 0.6 fusion.34
  128.1 1.9 collective-permute-start.3
  130.0 2.4 collective-permute-start.2
  132.4 1.6 copy.20
  134.0 2.0 add_convert_fusion
  136.1 2.3 fusion.4
  138.3 1.2 copy.19
  139.5 0.0 collective-permute-done.2
  139.5 0.8 fusion.24
  140.3 0.0 collective-permute-done.3
  140.3 0.8 fusion.23
  141.0 0.7 convert_element_type.58
  141.7 131.9 %reduce-scatter.4.cloned.1.call-done = f32[24,512]{1,0:T(8,128)} async-done(((f32[1536,512]{1,0:T(8,128)}), f32[24,512]{1,0:T(8,128)}) %reduce-scatter.4.cloned.1.call-update) | async-done | bytes 49168
  (4 shorter events, 0.0 us)
Async XLA Ops:
  7.2 15.7 %copy-start = (bf16[1536,512]{1,0:T(8,128)(2,1)S(1)}, bf16[1536,512]{1,0:T(8,128)(2,1)}, u32[]{:S(2)}) copy-start(bf16[1536,512]{1,0:T(8,128)(2,1)} %param.17) | copy-start | bytes 4718596
  7.2 13.7 %copy-start.3 = (bf16[768,512]{1,0:T(8,128)(2,1)S(1)}, bf16[768,512]{1,0:T(8,128)(2,1)}, u32[]{:S(2)}) copy-start(bf16[768,512]{1,0:T(8,128)(2,1)} %param.14) | copy-start | bytes 2359300
  7.2 14.8 %copy-start.4 = (bf16[768,512]{1,0:T(8,128)(2,1)S(1)}, bf16[768,512]{1,0:T(8,128)(2,1)}, u32[]{:S(2)}) copy-start(bf16[768,512]{1,0:T(8,128)(2,1)} %param.15) | copy-start | bytes 2359300
  7.2 112.0 %all-reduce.3.cloned.1.call-start = ((), (), s32[]{:S(2)}) async-start(), calls=%async_computation.1 | async-start | bytes 3145728 | tf_op jit(solution)/shard_map/psum | solution.py:107
  8.2 14.1 %collective-permute-start = (bf16[32,512]{1,0:T(8,128)(2,1)S(1)}, bf16[32,512]{1,0:T(8,128)(2,1)S(1)}, u32[]{:S(2)}, u32[]{:S(2)}) collective-permute-start(bf16[32,512]{1,0:T(8,128)(2,1)S(1)} %get-tuple-element.37), channel_id=1, source_target_pairs={{0,8},{8,16},{16,24},{24,32},{32,40},{40,48},{48,56},{56,64},{64,7... | collective-permute-start | bytes 98312 | tf_op jit(solution)/shard_map/ppermute | solution.py:16
  10.1 12.2 %collective-permute-start.1 = (bf16[32,512]{1,0:T(8,128)(2,1)S(1)}, bf16[32,512]{1,0:T(8,128)(2,1)S(1)}, u32[]{:S(2)}, u32[]{:S(2)}) collective-permute-start(bf16[32,512]{1,0:T(8,128)(2,1)S(1)} %get-tuple-element.38), channel_id=1, source_target_pairs={{8,0},{16,8},{24,16},{32,24},{40,32},{48,40},{56,48},{64,56},{72,6... | collective-permute-start | bytes 98312 | tf_op jit(solution)/shard_map/ppermute | solution.py:17
  20.8 1.5 copy-start.7
  22.9 2.9 %copy-start.10 = (bf16[512,512]{1,0:T(8,128)(2,1)S(1)}, bf16[512,512]{1,0:T(8,128)(2,1)}, u32[]{:S(2)}) copy-start(bf16[512,512]{1,0:T(8,128)(2,1)} %param.18) | copy-start | bytes 1572868
  26.5 0.9 copy-start.8
  26.5 0.9 copy-start.9
  28.2 1.2 copy-start.1
  29.4 1.1 copy-start.5
  29.4 1.4 copy-start.6
  33.3 240.3 %reduce-scatter.4.cloned.1.call-start = ((), (), s32[]{:S(2)}) async-start(), calls=%async_computation.2 | async-start | bytes 3194880
  124.2 2.1 copy-start.2
  128.1 12.2 %collective-permute-start.3 = (bf16[32,512]{1,0:T(8,128)(2,1)}, bf16[32,512]{1,0:T(8,128)(2,1)}, u32[]{:S(2)}, u32[]{:S(2)}) collective-permute-start(bf16[32,512]{1,0:T(8,128)(2,1)} %get-tuple-element.35), channel_id=1, source_target_pairs={{8,0},{16,8},{24,16},{32,24},{40,32},{48,40},{56,48},{64,56},{72,6... | collective-permute-start | bytes 98312 | tf_op jit(solution)/shard_map/ppermute | solution.py:25
  130.0 9.5 %collective-permute-start.2 = (bf16[32,512]{1,0:T(8,128)(2,1)}, bf16[32,512]{1,0:T(8,128)(2,1)}, u32[]{:S(2)}, u32[]{:S(2)}) collective-permute-start(bf16[32,512]{1,0:T(8,128)(2,1)} %get-tuple-element.36), channel_id=1, source_target_pairs={{504,0},{0,8},{8,16},{16,24},{24,32},{32,40},{40,48},{48,56},{56,6... | collective-permute-start | bytes 98312 | tf_op jit(solution)/shard_map/ppermute | solution.py:25
Sparse Core Ops, SparseCore 0:
  33.4 85.7 all-reduce.2
  124.5 149.0 reduce-scatter.3
where the time goes:
time: 282 us; the launch traced here: 280 us
  waiting for transfers between devices  218 us (77%)
  matrix products  15.6 us (6%)
  between operations  15 us (5%)
  starting transfers between devices  13.3 us (5%)
  local copies, waits for them, and re-layouts  10.1 us (4%)
  other arithmetic  8.66 us (3%)
    unnamed x3, waiting for transfers between devices  132 us
    psum x1, waiting for transfers between devices, per_device(): lax.psum(local_weight.astype(jnp.bfloat16), 'band').astype(jnp.float32)  85.9 us
    unnamed x26, local copies, waits for them, and re-layouts  8.43 us
    ppermute x1, starting transfers between devices, with_halo(): after = lax.ppermute(leading, axis, down)  7.01 us
  transfers between devices with their start and end apart: 6, of which 2 were waited for; matrix products, arithmetic and copies ran while one was open for 6% of the time, Pallas kernels for 0%

commit v1 on v0

v1 whole, which is shorter than its diff:
```python
import itertools

import jax
import jax.numpy as jnp
from jax import lax
from jax.experimental import pallas as pl
from jax.experimental.pallas import tpu as pltpu
from jax.sharding import PartitionSpec as P

HALO = 32
ROWS = 128
SLOTS = 768
WIDTH = 512
BLOCK = 256
AXES = ("patch", "band")
BF16 = jnp.bfloat16
F32 = jnp.float32


def device_groups(y_parts, x_parts, z_parts):
    groups = []
    for ys, xs, zs, core in itertools.product(y_parts, x_parts, z_parts, range(2)):
        groups.append(
            [((y * 4 + x) * 2 + core) * 8 + z for x, y, z in itertools.product(xs, ys, zs)]
        )
    return groups


SINGLE_X, SINGLE_Y, SINGLE_Z = ([[i] for i in range(n)] for n in (4, 8, 8))
X_AND_Y_PAIR = device_groups([[2 * i, 2 * i + 1] for i in range(4)], [list(range(4))], SINGLE_Z)
Y_QUADS = device_groups([[0, 2, 4, 6], [1, 3, 5, 7]], SINGLE_X, SINGLE_Z)
Z_ALL = device_groups(SINGLE_Y, SINGLE_X, [list(range(8))])
PAIR = [(i, i ^ 1) for i in range(64)]
CROSS = [(i, (i - 1) % 64 if i % 2 == 0 else (i + 1) % 64) for i in range(64)]


def dot(a, b, dims):
    return lax.dot_general(a, b, (dims, ((), ())), preferred_element_type=F32)


NN = ((1,), (0,))
NT = ((1,), (1,))
TN = ((0,), (0,))


def kernel(
    scalars,
    senders,
    receivers,
    nodes,
    pair,
    cross,
    edges,
    d_new,
    d_agg,
    w1,
    w2,
    mine,
    theirs,
    d_edges,
    node_grad,
    ret_pair,
    ret_cross,
    dz_all,
    scatter,
    table,
    weight,
):
    here, odd, count = scalars[0], scalars[1], scalars[2]
    table[:ROWS] = nodes[...]
    table[ROWS : ROWS + HALO] = pair[...]
    table[ROWS + HALO :] = cross[...]
    owner = senders[...] // (ROWS * 8)
    offset = senders[...] % ROWS
    lower = jnp.where(here == 0, 63, here - 1)
    lower_base = jnp.where(odd == 1, ROWS, ROWS + HALO) - (ROWS - HALO)
    upper_base = jnp.where(odd == 1, ROWS + HALO, ROWS)
    position = jnp.where(
        owner == here, offset, jnp.where(owner == lower, lower_base + offset, upper_base + offset)
    )
    receive = receivers[...]

    def columns(index, part):
        row = jnp.broadcast_to(index[part : part + 1, :], (128, 128))
        return row.T

    def hot(mask):
        return jnp.where(mask, 1.0, 0.0).astype(BF16)

    lane = lax.broadcasted_iota(jnp.int32, (128, 128), 1)
    wide = lax.broadcasted_iota(jnp.int32, (128, 64), 1)
    for start in range(0, SLOTS, BLOCK):
        send_hot, recv_hot = [], []
        for part in range(start // 128, (start + BLOCK) // 128):
            place = columns(position, part)
            send_hot.append(
                jnp.concatenate([hot(place == lane), hot(place[:, :64] == wide + 128)], axis=1)
            )
            recv_hot.append(hot(columns(receive, part) == lane))
            row = pl.ds(part * 128, 128)
            scatter[: ROWS + 2 * HALO, row] = hot(
                lax.broadcasted_iota(jnp.int32, (192, 128), 0) == position[part : part + 1, :]
            )
            scatter[ROWS + 2 * HALO :, row] = hot(
                lax.broadcasted_iota(jnp.int32, (128, 128), 0) == receive[part : part + 1, :]
            )
        send_hot = jnp.concatenate(send_hot, axis=0)
        recv_hot = jnp.concatenate(recv_hot, axis=0)
        rows = pl.ds(start, BLOCK)
        sent = dot(send_hot, table[...], NN).astype(BF16)
        got = dot(recv_hot, nodes[...], NN).astype(BF16)
        pre = (
            dot(edges[rows, :], w1[:WIDTH], NN)
            + dot(sent, w1[WIDTH : 2 * WIDTH], NN)
            + dot(got, w1[2 * WIDTH :], NN)
        )
        sigma = 0.5 * jnp.tanh(0.5 * pre) + 0.5
        hidden = (pre * sigma).astype(BF16)
        out = dot(hidden, w2[...], NN)
        center = out - jnp.mean(out, axis=-1, keepdims=True)
        rstd = lax.rsqrt(jnp.mean(center * center, axis=-1, keepdims=True) + 1e-05)
        normed = center * rstd
        slot = start + lax.broadcasted_iota(jnp.int32, (BLOCK, 1), 0)
        live = jnp.where(slot < count, 1.0, 0.0)
        grad_new = live * (d_new[rows, :].astype(F32) + dot(recv_hot, d_agg[...], NN))
        g_out = (
            grad_new
            - jnp.mean(grad_new, axis=-1, keepdims=True)
            - normed * jnp.mean(grad_new * normed, axis=-1, keepdims=True)
        ) * rstd
        g_hidden = dot(g_out.astype(BF16), w2[...], NT)
        dz = (g_hidden * (sigma * (1.0 + pre * (1.0 - sigma)))).astype(BF16)
        dz_all[rows, :] = dz
        d_edges[rows, :] = (grad_new + dot(dz, w1[:WIDTH], NT)).astype(BF16)

    dz = dz_all[...]
    summed = dot(scatter[...], dz, NN).astype(BF16)
    by_sender, by_receiver = summed[: ROWS + 2 * HALO], summed[ROWS + 2 * HALO :]
    weight[:WIDTH] = dot(edges[...], dz, TN)
    weight[WIDTH : 2 * WIDTH] = dot(table[...], by_sender, TN)
    weight[2 * WIDTH :] = dot(nodes[...], by_receiver, TN)

    def arrange(core, target):
        for x, y in itertools.product(range(4), range(2)):
            pieces = []
            for quad in range(4):
                first = ((quad * 2 + y) * 4 + x) * 48 + core * 24
                pieces.append(weight[first : first + 24, :])
            place = (x * 2 + y) * 96
            target[place : place + 96, :] = jnp.concatenate(pieces, axis=0).astype(BF16)

    @pl.when(odd == 0)
    def _():
        arrange(0, mine)
        arrange(1, theirs)

    @pl.when(odd == 1)
    def _():
        arrange(1, mine)
        arrange(0, theirs)

    sender_grad = dot(by_sender, w1[WIDTH : 2 * WIDTH], NT)
    node_grad[...] = sender_grad[:ROWS] + dot(by_receiver, w1[2 * WIDTH :], NT)
    ret_pair[...] = sender_grad[ROWS : ROWS + HALO].astype(BF16)
    ret_cross[...] = sender_grad[ROWS + HALO :].astype(BF16)


def local_grads(*args):
    shapes = (
        ((SLOTS, WIDTH), BF16),
        ((SLOTS, WIDTH), BF16),
        ((SLOTS, WIDTH), BF16),
        ((ROWS, WIDTH), F32),
        ((HALO, WIDTH), BF16),
        ((HALO, WIDTH), BF16),
    )
    vmem = pl.BlockSpec(memory_space=pltpu.VMEM)
    return pl.pallas_call(
        kernel,
        out_shape=[jax.ShapeDtypeStruct(s, d) for s, d in shapes],
        in_specs=[pl.BlockSpec(memory_space=pltpu.SMEM)] + [vmem] * 10,
        out_specs=[vmem] * 6,
        scratch_shapes=[
            pltpu.VMEM((SLOTS, WIDTH), BF16),
            pltpu.VMEM((2 * ROWS + 2 * HALO, SLOTS), BF16),
            pltpu.VMEM((ROWS + 2 * HALO, WIDTH), BF16),
            pltpu.VMEM((3 * WIDTH, WIDTH), F32),
        ],
        compiler_params=pltpu.CompilerParams(vmem_limit_bytes=48 * 1024 * 1024),
        cost_estimate=pl.CostEstimate(
            flops=6_000_000_000, bytes_accessed=8_000_000, transcendentals=400_000
        ),
    )(*args)


def exchange(block, groups):
    return lax.all_to_all(block, AXES, 0, 0, axis_index_groups=groups)


def total(block):
    return jnp.sum(block.astype(F32), axis=0)


def per_device(
    nodes, edges, d_new_edges, d_aggregate, edge_w1, edge_w2, senders, receivers, edge_count
):
    here = lax.axis_index("patch")
    odd = here % 2
    first = nodes[:HALO]
    last = nodes[ROWS - HALO :]
    pair = lax.ppermute(jnp.where(odd == 0, last, first), "patch", PAIR)
    cross = lax.ppermute(jnp.where(odd == 0, first, last), "patch", CROSS)
    scalars = jnp.stack([here, odd, edge_count[0]]).astype(jnp.int32)
    mine, theirs, edge_grad, node_grad, ret_pair, ret_cross = local_grads(
        scalars,
        senders.reshape(6, 128),
        receivers.reshape(6, 128),
        nodes,
        pair,
        cross,
        edges,
        d_new_edges,
        d_aggregate,
        edge_w1,
        edge_w2,
    )
    other = lax.ppermute(theirs, "patch", PAIR)
    from_pair = lax.ppermute(ret_pair, "patch", PAIR).astype(F32)
    from_cross = lax.ppermute(ret_cross, "patch", CROSS).astype(F32)
    weight = (mine.astype(F32) + other.astype(F32)).astype(BF16).reshape(8, 96, WIDTH)
    weight = total(exchange(weight, X_AND_Y_PAIR)).astype(BF16).reshape(4, 24, WIDTH)
    weight = total(exchange(weight, Y_QUADS)).astype(BF16)
    weight = jnp.broadcast_to(weight[None], (8, 24, WIDTH))
    weight_grad = total(exchange(weight, Z_ALL))
    from_lower = jnp.where(odd == 1, from_pair, from_cross)
    from_upper = jnp.where(odd == 1, from_cross, from_pair)
    gap = jnp.zeros((ROWS - 2 * HALO, WIDTH), F32)
    node_grad = node_grad + jnp.concatenate([from_lower, gap, from_upper], axis=0)
    return (node_grad.astype(BF16), edge_grad, weight_grad)


def solution(mesh):
    placed = (
        P(AXES, None),
        P(AXES, None),
        P(AXES, None),
        P(AXES, None),
        P(),
        P(),
        P(AXES),
        P(AXES),
        P(AXES),
    )
    return jax.shard_map(
        per_device,
        mesh=mesh,
        in_specs=placed,
        out_specs=(P(AXES, None), P(AXES, None), P("patch", None)),
        check_vma=False,
    )
```

time: 282 us -> 83.5 us (0.30)
  the two profiles are of different devices: /device:TPU:64 before, /device:TPU:8 now
where the time goes in v1:
time: 83.5 us; the launch traced here: 82.7 us
  starting transfers between devices  25.1 us (30%)
  blocking collectives  21.8 us (26%)
  waiting for transfers between devices  15 us (18%)
  local copies, waits for them, and re-layouts  8.67 us (10%)
  Pallas kernels  7.49 us (9%)
  other arithmetic  3.28 us (4%)
  between operations  1.39 us (2%)
    all_to_all x1, blocking collectives, exchange(): return lax.all_to_all(block, AXES, 0, 0, axis_index_groups=groups)  21.8 us
    all_to_all x2, waiting for transfers between devices, exchange(): return lax.all_to_all(block, AXES, 0, 0, axis_index_groups=groups)  12.1 us
    all_to_all x2, starting transfers between devices, exchange(): return lax.all_to_all(block, AXES, 0, 0, axis_index_groups=groups)  11.9 us
    unnamed x16, local copies, waits for them, and re-layouts  7.9 us
    pallas_call x1, Pallas kernels, local_grads(): pl.pallas_call(kernel, out_shape=[jax.ShapeDtypeStruct(s, d) for s, d in...  7.49 us
    ppermute x1, starting transfers between devices, per_device(): cross = lax.ppermute(jnp.where(odd == 0, first, last), 'patch', CROSS)  3.98 us
    ppermute x1, starting transfers between devices, per_device(): from_cross = lax.ppermute(ret_cross, 'patch', CROSS).astype(F32)  3.47 us
    ppermute x1, waiting for transfers between devices, per_device(): other = lax.ppermute(theirs, 'patch', PAIR)  2.25 us
  transfers between devices with their start and end apart: 7, of which 4 were waited for; matrix products, arithmetic and copies ran while one was open for 2% of the time, Pallas kernels for 0%

profile of v1, /device:TPU:8, one launch (start us, length us, event | category | flops | bytes accessed | tf_op | source)
XLA Modules:
  0.0 82.7 jit_solution(4998395072250637006)
XLA Ops:
  0.6 0.8 broadcast_select_fusion
  1.4 4.0 %collective-permute-start.1 = (bf16[32,512]{1,0:T(8,128)(2,1)S(1)}, bf16[32,512]{1,0:T(8,128)(2,1)S(1)}, u32[]{:S(2)}, u32[]{:S(2)}) collective-permute-start(bf16[32,512]{1,0:T(8,128)(2,1)S(1)} %get-tuple-element.15), channel_id=1, source_target_pairs={{0,504},{8,16},{16,8},{24,32},{32,24},{40,48},{48,40},{56,64},{64,... | collective-permute-start | bytes 98312 | tf_op jit(solution)/shard_map/ppermute | solution.py:212
  5.4 1.9 %collective-permute-start = (bf16[32,512]{1,0:T(8,128)(2,1)S(1)}, bf16[32,512]{1,0:T(8,128)(2,1)S(1)}, u32[]{:S(2)}, u32[]{:S(2)}) collective-permute-start(bf16[32,512]{1,0:T(8,128)(2,1)S(1)} %get-tuple-element.16), channel_id=1, source_target_pairs={{0,8},{8,0},{16,24},{24,16},{32,40},{40,32},{48,56},{56,48},{64,72... | collective-permute-start | bytes 98312 | tf_op jit(solution)/shard_map/ppermute | solution.py:211
  8.0 0.1 pad_add_fusion.scalars
  8.1 0.7 collective-permute-done.1.cross
  8.8 0.0 collective-permute-done.pair
  8.8 0.0 copy-start
  8.8 0.9 %copy-done = bf16[128,512]{1,0:T(8,128)(2,1)S(1)} copy-done((bf16[128,512]{1,0:T(8,128)(2,1)S(1)}, bf16[128,512]{1,0:T(8,128)(2,1)}, u32[]{:S(2)}) %copy-start) | copy-done | bytes 131096
  9.7 0.0 copy-start.1
  9.7 1.4 %copy-done.1 = bf16[1536,512]{1,0:T(8,128)(2,1)S(1)} copy-done((bf16[1536,512]{1,0:T(8,128)(2,1)S(1)}, bf16[1536,512]{1,0:T(8,128)(2,1)}, u32[]{:S(2)}) %copy-start.1) | copy-done | bytes 1572888
  11.1 0.0 copy-start.2
  11.1 1.1 %copy-done.2 = bf16[768,512]{1,0:T(8,128)(2,1)S(1)} copy-done((bf16[768,512]{1,0:T(8,128)(2,1)S(1)}, bf16[768,512]{1,0:T(8,128)(2,1)}, u32[]{:S(2)}) %copy-start.2) | copy-done | bytes 786456
  12.2 0.0 copy-start.3
  12.2 1.1 %copy-done.3 = bf16[768,512]{1,0:T(8,128)(2,1)S(1)} copy-done((bf16[768,512]{1,0:T(8,128)(2,1)S(1)}, bf16[768,512]{1,0:T(8,128)(2,1)}, u32[]{:S(2)}) %copy-start.3) | copy-done | bytes 786456
  13.3 0.0 copy-start.4
  13.4 1.0 %copy-done.4 = bf16[512,512]{1,0:T(8,128)(2,1)S(1)} copy-done((bf16[512,512]{1,0:T(8,128)(2,1)S(1)}, bf16[512,512]{1,0:T(8,128)(2,1)}, u32[]{:S(2)}) %copy-start.4) | copy-done | bytes 524312
  14.4 0.0 copy-start.5
  14.4 0.9 %copy-done.5 = bf16[128,512]{1,0:T(8,128)(2,1)S(1)} copy-done((bf16[128,512]{1,0:T(8,128)(2,1)S(1)}, bf16[128,512]{1,0:T(8,128)(2,1)}, u32[]{:S(2)}) %copy-start.5) | copy-done | bytes 131096
  15.3 0.0 copy-start.6
  15.3 0.7 copy-done.6
  16.0 0.0 copy-start.7
  16.0 0.7 copy-done.7
  16.7 7.5 %shard_map.112 = (bf16[768,512]{1,0:T(8,128)(2,1)S(1)}, bf16[768,512]{1,0:T(8,128)(2,1)S(1)}, bf16[768,512]{1,0:T(8,128)(2,1)}, f32[128,512]{1,0:T(8,128)S(1)}, ...) custom-call(s32[3]{0:T(128)S(1)} %pad_add_fusion.scalars, s32[6,128]{1,0:T(8,128)S(1)} %bitcast.6, ...), custom_call_target="tpu_custom_call" | custom-call | flops 6000000000 | bytes 8000000 | tf_op jit(solution)/shard_map/pallas_call | solution.py:178
  24.2 1.9 %collective-permute-start.4 = (bf16[768,512]{1,0:T(8,128)(2,1)S(1)}, bf16[768,512]{1,0:T(8,128)(2,1)S(1)}, u32[]{:S(2)}, u32[]{:S(2)}) collective-permute-start(bf16[768,512]{1,0:T(8,128)(2,1)S(1)} %get-tuple-element.14), channel_id=1, source_target_pairs={{0,8},{8,0},{16,24},{24,16},{32,40},{40,32},{48,56},{56,48},{64,72... | collective-permute-start | bytes 2359304 | tf_op jit(solution)/shard_map/ppermute | solution.py:227
  26.1 2.3 %collective-permute-done.4 = bf16[768,512]{1,0:T(8,128)(2,1)S(1)} collective-permute-done((bf16[768,512]{1,0:T(8,128)(2,1)S(1)}, bf16[768,512]{1,0:T(8,128)(2,1)S(1)}, u32[]{:S(2)}, u32[]{:S(2)}) %collective-permute-start.4) | collective-permute-done | bytes 786464 | tf_op jit(solution)/shard_map/ppermute | solution.py:227
  28.3 0.2 add_convert_fusion
  28.6 21.8 %all_to_all.15 = bf16[8,96,512]{2,1,0:T(8,128)(2,1)S(1)} all-to-all(bf16[8,96,512]{2,1,0:T(8,128)(2,1)S(1)} %bitcast.8), channel_id=1, replica_groups={{0,64,16,80,32,96,48,112},{8,72,24,88,40,104,56,120},{1,65,17,81,33,97,..., dimensions={0} | all-to-all | bytes 1572864 | tf_op jit(solution)/shard_map/all_to_all | solution.py:197
  50.3 0.8 reduce_sum.33
  51.1 3.3 %all-to-all-start.1 = ((bf16[4,24,512]{2,1,0:T(8,128)(2,1)}), bf16[4,24,512]{2,1,0:T(8,128)(2,1)S(1)}, u32[]{:S(2)}, u32[]{:S(2)}) async-start(bf16[4,24,512]{2,1,0:T(8,128)(2,1)} %bitcast.5), calls=%async_computation.1 | async-start | bytes 196608 | tf_op jit(solution)/shard_map/all_to_all | solution.py:197
  54.4 1.9 %collective-permute-start.2 = (bf16[32,512]{1,0:T(8,128)(2,1)S(1)}, bf16[32,512]{1,0:T(8,128)(2,1)S(1)}, u32[]{:S(2)}, u32[]{:S(2)}) collective-permute-start(bf16[32,512]{1,0:T(8,128)(2,1)S(1)} %get-tuple-element.10), channel_id=1, source_target_pairs={{0,8},{8,0},{16,24},{24,16},{32,40},{40,32},{48,56},{56,48},{64,72... | collective-permute-start | bytes 98312 | tf_op jit(solution)/shard_map/ppermute | solution.py:228
  56.3 3.5 %collective-permute-start.3 = (bf16[32,512]{1,0:T(8,128)(2,1)S(1)}, bf16[32,512]{1,0:T(8,128)(2,1)S(1)}, u32[]{:S(2)}, u32[]{:S(2)}) collective-permute-start(bf16[32,512]{1,0:T(8,128)(2,1)S(1)} %get-tuple-element.11), channel_id=1, source_target_pairs={{0,504},{8,16},{16,8},{24,32},{32,24},{40,48},{48,40},{56,64},{64,... | collective-permute-start | bytes 98312 | tf_op jit(solution)/shard_map/ppermute | solution.py:229
  59.8 0.1 pad.1.clone
  59.9 3.1 %all-to-all-done.1 = bf16[4,24,512]{2,1,0:T(8,128)(2,1)S(1)} async-done(((bf16[4,24,512]{2,1,0:T(8,128)(2,1)}), bf16[4,24,512]{2,1,0:T(8,128)(2,1)S(1)}, u32[]{:S(2)}, u32[]{:S(2)}) %all-to-all-start.1) | async-done | bytes 98336 | tf_op jit(solution)/shard_map/all_to_all | solution.py:197
  63.0 0.7 broadcast_in_dim.10
  63.7 8.6 %all-to-all-start.2 = ((bf16[8,24,512]{2,1,0:T(8,128)(2,1)}), bf16[8,24,512]{2,1,0:T(8,128)(2,1)S(1)}, u32[]{:S(2)}, u32[]{:S(2)}) async-start(bf16[8,24,512]{2,1,0:T(8,128)(2,1)} %broadcast_in_dim.10), calls=%async_computation.2 | async-start | bytes 393216 | tf_op jit(solution)/shard_map/all_to_all | solution.py:197
  72.3 0.0 collective-permute-done.2
  72.3 0.0 collective-permute-done.3
  72.3 0.7 fusion
  73.1 9.0 %all-to-all-done.2 = bf16[8,24,512]{2,1,0:T(8,128)(2,1)S(1)} async-done(((bf16[8,24,512]{2,1,0:T(8,128)(2,1)}), bf16[8,24,512]{2,1,0:T(8,128)(2,1)S(1)}, u32[]{:S(2)}, u32[]{:S(2)}) %all-to-all-start.2) | async-done | bytes 196640 | tf_op jit(solution)/shard_map/all_to_all | solution.py:197
  82.1 0.6 convert_reduce_fusion
  (3 shorter events, 0.0 us)
Async XLA Ops:
  1.4 7.3 %collective-permute-start.1 = (bf16[32,512]{1,0:T(8,128)(2,1)S(1)}, bf16[32,512]{1,0:T(8,128)(2,1)S(1)}, u32[]{:S(2)}, u32[]{:S(2)}) collective-permute-start(bf16[32,512]{1,0:T(8,128)(2,1)S(1)} %get-tuple-element.15), channel_id=1, source_target_pairs={{0,504},{8,16},{16,8},{24,32},{32,24},{40,48},{48,40},{56,64},{64,... | collective-permute-start | bytes 98312 | tf_op jit(solution)/shard_map/ppermute | solution.py:212
  5.4 3.3 %collective-permute-start = (bf16[32,512]{1,0:T(8,128)(2,1)S(1)}, bf16[32,512]{1,0:T(8,128)(2,1)S(1)}, u32[]{:S(2)}, u32[]{:S(2)}) collective-permute-start(bf16[32,512]{1,0:T(8,128)(2,1)S(1)} %get-tuple-element.16), channel_id=1, source_target_pairs={{0,8},{8,0},{16,24},{24,16},{32,40},{40,32},{48,56},{56,48},{64,72... | collective-permute-start | bytes 98312 | tf_op jit(solution)/shard_map/ppermute | solution.py:211
  8.8 0.9 %copy-start = (bf16[128,512]{1,0:T(8,128)(2,1)S(1)}, bf16[128,512]{1,0:T(8,128)(2,1)}, u32[]{:S(2)}) copy-start(bf16[128,512]{1,0:T(8,128)(2,1)} %nodes.1) | copy-start | bytes 393220
  9.7 1.4 %copy-start.1 = (bf16[1536,512]{1,0:T(8,128)(2,1)S(1)}, bf16[1536,512]{1,0:T(8,128)(2,1)}, u32[]{:S(2)}) copy-start(bf16[1536,512]{1,0:T(8,128)(2,1)} %w1.1) | copy-start | bytes 4718596
  11.1 1.1 %copy-start.2 = (bf16[768,512]{1,0:T(8,128)(2,1)S(1)}, bf16[768,512]{1,0:T(8,128)(2,1)}, u32[]{:S(2)}) copy-start(bf16[768,512]{1,0:T(8,128)(2,1)} %edges.1) | copy-start | bytes 2359300
  12.2 1.1 %copy-start.3 = (bf16[768,512]{1,0:T(8,128)(2,1)S(1)}, bf16[768,512]{1,0:T(8,128)(2,1)}, u32[]{:S(2)}) copy-start(bf16[768,512]{1,0:T(8,128)(2,1)} %d_new.1) | copy-start | bytes 2359300
  13.3 1.0 %copy-start.4 = (bf16[512,512]{1,0:T(8,128)(2,1)S(1)}, bf16[512,512]{1,0:T(8,128)(2,1)}, u32[]{:S(2)}) copy-start(bf16[512,512]{1,0:T(8,128)(2,1)} %w2.1) | copy-start | bytes 1572868
  14.4 0.9 %copy-start.5 = (bf16[128,512]{1,0:T(8,128)(2,1)S(1)}, bf16[128,512]{1,0:T(8,128)(2,1)}, u32[]{:S(2)}) copy-start(bf16[128,512]{1,0:T(8,128)(2,1)} %d_agg.1) | copy-start | bytes 393220
  15.3 0.7 copy-start.6
  16.0 0.7 copy-start.7
  24.2 4.2 %collective-permute-start.4 = (bf16[768,512]{1,0:T(8,128)(2,1)S(1)}, bf16[768,512]{1,0:T(8,128)(2,1)S(1)}, u32[]{:S(2)}, u32[]{:S(2)}) collective-permute-start(bf16[768,512]{1,0:T(8,128)(2,1)S(1)} %get-tuple-element.14), channel_id=1, source_target_pairs={{0,8},{8,0},{16,24},{24,16},{32,40},{40,32},{48,56},{56,48},{64,72... | collective-permute-start | bytes 2359304 | tf_op jit(solution)/shard_map/ppermute | solution.py:227
  51.1 11.9 %all-to-all-start.1 = ((bf16[4,24,512]{2,1,0:T(8,128)(2,1)}), bf16[4,24,512]{2,1,0:T(8,128)(2,1)S(1)}, u32[]{:S(2)}, u32[]{:S(2)}) async-start(bf16[4,24,512]{2,1,0:T(8,128)(2,1)} %bitcast.5), calls=%async_computation.1 | async-start | bytes 196608 | tf_op jit(solution)/shard_map/all_to_all | solution.py:197
  54.4 17.9 %collective-permute-start.2 = (bf16[32,512]{1,0:T(8,128)(2,1)S(1)}, bf16[32,512]{1,0:T(8,128)(2,1)S(1)}, u32[]{:S(2)}, u32[]{:S(2)}) collective-permute-start(bf16[32,512]{1,0:T(8,128)(2,1)S(1)} %get-tuple-element.10), channel_id=1, source_target_pairs={{0,8},{8,0},{16,24},{24,16},{32,40},{40,32},{48,56},{56,48},{64,72... | collective-permute-start | bytes 98312 | tf_op jit(solution)/shard_map/ppermute | solution.py:228
  56.3 16.0 %collective-permute-start.3 = (bf16[32,512]{1,0:T(8,128)(2,1)S(1)}, bf16[32,512]{1,0:T(8,128)(2,1)S(1)}, u32[]{:S(2)}, u32[]{:S(2)}) collective-permute-start(bf16[32,512]{1,0:T(8,128)(2,1)S(1)} %get-tuple-element.11), channel_id=1, source_target_pairs={{0,504},{8,16},{16,8},{24,32},{32,24},{40,48},{48,40},{56,64},{64,... | collective-permute-start | bytes 98312 | tf_op jit(solution)/shard_map/ppermute | solution.py:229
  63.7 18.4 %all-to-all-start.2 = ((bf16[8,24,512]{2,1,0:T(8,128)(2,1)}), bf16[8,24,512]{2,1,0:T(8,128)(2,1)S(1)}, u32[]{:S(2)}, u32[]{:S(2)}) async-start(bf16[8,24,512]{2,1,0:T(8,128)(2,1)} %broadcast_in_dim.10), calls=%async_computation.2 | async-start | bytes 393216 | tf_op jit(solution)/shard_map/all_to_all | solution.py:197

commit v2 on v1

v2 whole, which is shorter than its diff:
```python
import itertools

import jax
import jax.numpy as jnp
from jax import lax
from jax.experimental import pallas as pl
from jax.experimental.pallas import tpu as pltpu
from jax.sharding import PartitionSpec as P

HALO = 32
ROWS = 128
SLOTS = 768
WIDTH = 512
PLACES = 2 * ROWS + 2 * HALO
BLOCK = 768
AXES = ("patch", "band")
BF16 = jnp.bfloat16
F32 = jnp.float32
VMEM = pl.BlockSpec(memory_space=pltpu.VMEM)
SMEM = pl.BlockSpec(memory_space=pltpu.SMEM)
HBM = pl.BlockSpec(memory_space=pl.ANY)


def device_groups(y_parts, x_parts, z_parts):
    groups = []
    for ys, xs, zs, core in itertools.product(y_parts, x_parts, z_parts, range(2)):
        groups.append(
            [((y * 4 + x) * 2 + core) * 8 + z for x, y, z in itertools.product(xs, ys, zs)]
        )
    return groups


SINGLE_X, SINGLE_Y, SINGLE_Z = ([[i] for i in range(n)] for n in (4, 8, 8))
X_AND_Y_PAIR = device_groups([[2 * i, 2 * i + 1] for i in range(4)], [list(range(4))], SINGLE_Z)
Y_QUADS = device_groups([[0, 2, 4, 6], [1, 3, 5, 7]], SINGLE_X, SINGLE_Z)
Z_ALL = device_groups(SINGLE_Y, SINGLE_X, [list(range(8))])
PAIR = [(i, i ^ 1) for i in range(64)]
CROSS = [(i, (i - 1) % 64 if i % 2 == 0 else (i + 1) % 64) for i in range(64)]

NN = ((1,), (0,))
NT = ((1,), (1,))
TN = ((0,), (0,))


def dot(a, b, dims=NN):
    return lax.dot_general(a, b, (dims, ((), ())), preferred_element_type=F32)


def hot(mask):
    return jnp.where(mask, 1.0, 0.0).astype(BF16)


def halves(values):
    high = values.astype(BF16)
    return jnp.concatenate([high, (values - high.astype(F32)).astype(BF16)], axis=0)


def prepare_kernel(
    scalars,
    senders_hbm,
    receivers_hbm,
    nodes_hbm,
    edges_hbm,
    d_new_hbm,
    d_agg_hbm,
    w1_hbm,
    w2_hbm,
    base,
    grad_new,
    edges_t,
    scatter,
    halo_hot,
    w1,
    w2,
    nodes,
    edges,
    d_new,
    d_agg,
    senders,
    receivers,
    sems,
):
    pairs = (
        (senders_hbm, senders),
        (receivers_hbm, receivers),
        (nodes_hbm, nodes),
        (w1_hbm, w1),
        (edges_hbm, edges),
        (d_agg_hbm, d_agg),
        (d_new_hbm, d_new),
        (w2_hbm, w2),
    )
    copies = [pltpu.make_async_copy(a, b, sems.at[i]) for i, (a, b) in enumerate(pairs)]
    for copy in copies:
        copy.start()
    here, odd, count = scalars[0], scalars[1], scalars[2]
    copies[0].wait()
    copies[1].wait()
    owner = senders[...] // (ROWS * 8)
    offset = senders[...] % ROWS
    lower = jnp.where(here == 0, 63, here - 1)
    lower_base = jnp.where(odd == 1, ROWS, ROWS + HALO) - (ROWS - HALO)
    upper_base = jnp.where(odd == 1, ROWS + HALO, ROWS)
    position = jnp.where(
        owner == here, offset, jnp.where(owner == lower, lower_base + offset, upper_base + offset)
    )
    receive = receivers[...]

    def columns(index, part):
        return jnp.broadcast_to(index[part : part + 1, :], (128, 128)).T

    lane = lax.broadcasted_iota(jnp.int32, (128, 128), 1)
    send_hot, recv_hot = [], []
    for part in range(SLOTS // 128):
        place = columns(position, part)
        send_hot.append(hot(place == lane))
        halo_hot[part * 128 : part * 128 + 128, :] = hot(place == ROWS + lane % 64)
        recv_hot.append(hot(columns(receive, part) == lane))
        row = slice(part * 128, part * 128 + 128)
        scatter[: ROWS + 2 * HALO, row] = hot(
            lax.broadcasted_iota(jnp.int32, (192, 128), 0) == position[part : part + 1, :]
        )
        scatter[ROWS + 2 * HALO :, row] = hot(
            lax.broadcasted_iota(jnp.int32, (128, 128), 0) == receive[part : part + 1, :]
        )
    copies[2].wait()
    copies[3].wait()
    product = jnp.concatenate(
        [
            halves(dot(nodes[...], w1[WIDTH : 2 * WIDTH])),
            halves(dot(nodes[...], w1[2 * WIDTH :])),
        ],
        axis=0,
    )
    copies[4].wait()
    for start in range(0, SLOTS, BLOCK):
        rows = slice(start, start + BLOCK)
        parts = range(start // 128, (start + BLOCK) // 128)
        gather = jnp.concatenate(
            [
                jnp.concatenate([send_hot[p], send_hot[p], recv_hot[p], recv_hot[p]], axis=1)
                for p in parts
            ],
            axis=0,
        )
        base[rows, :] = dot(edges[rows, :], w1[:WIDTH]) + dot(gather, product)
        edges_t[:, rows] = edges[rows, :].T
    copies[5].wait()
    copies[6].wait()
    for start in range(0, SLOTS, BLOCK):
        rows = slice(start, start + BLOCK)
        parts = range(start // 128, (start + BLOCK) // 128)
        slot = start + lax.broadcasted_iota(jnp.int32, (BLOCK, 1), 0)
        live = jnp.where(slot < count, 1.0, 0.0)
        taken = dot(jnp.concatenate([recv_hot[p] for p in parts], axis=0), d_agg[...])
        grad_new[rows, :] = live * (d_new[rows, :].astype(F32) + taken)
    copies[7].wait()


def prepare(*args):
    shapes = (
        ((SLOTS, WIDTH), F32),
        ((SLOTS, WIDTH), F32),
        ((WIDTH, SLOTS), BF16),
        ((PLACES, SLOTS), BF16),
        ((SLOTS, 128), BF16),
        ((3 * WIDTH, WIDTH), BF16),
        ((WIDTH, WIDTH), BF16),
        ((ROWS, WIDTH), BF16),
    )
    args = args[:1] + tuple(pltpu.with_memory_space_constraint(a, pltpu.HBM) for a in args[1:])
    return pl.pallas_call(
        prepare_kernel,
        out_shape=[pltpu.VMEM(s, d) for s, d in shapes],
        in_specs=[SMEM] + [HBM] * 8,
        out_specs=[VMEM] * 8,
        scratch_shapes=[
            pltpu.VMEM((SLOTS, WIDTH), BF16),
            pltpu.VMEM((SLOTS, WIDTH), BF16),
            pltpu.VMEM((ROWS, WIDTH), BF16),
            pltpu.VMEM((6, 128), jnp.int32),
            pltpu.VMEM((6, 128), jnp.int32),
            pltpu.SemaphoreType.DMA((8,)),
        ],
        compiler_params=pltpu.CompilerParams(vmem_limit_bytes=20 * 1024 * 1024),
        cost_estimate=pl.CostEstimate(
            flops=2_000_000_000, bytes_accessed=10_000_000, transcendentals=0
        ),
    )(*args)


def weight_kernel(
    scalars,
    pair,
    cross,
    base,
    grad_new,
    edges_t,
    scatter,
    halo_hot,
    w1,
    w2,
    nodes,
    mine,
    theirs,
    dz_all,
    summed,
    ret_cross,
    weight,
):
    odd = scalars[1]
    halo = jnp.concatenate([pair[...], cross[...]], axis=0)
    halo_product = halves(dot(halo, w1[WIDTH : 2 * WIDTH]))
    for start in range(0, SLOTS, BLOCK):
        rows = slice(start, start + BLOCK)
        pre = base[rows, :] + dot(halo_hot[rows, :], halo_product)
        sigma = 0.5 * jnp.tanh(0.5 * pre) + 0.5
        hidden = pre * sigma
        out = dot(hidden.astype(BF16), w2[...])
        center = out - jnp.mean(out, axis=-1, keepdims=True)
        rstd = lax.rsqrt(jnp.mean(center * center, axis=-1, keepdims=True) + 1e-05)
        normed = center * rstd
        grad = grad_new[rows, :]
        g_out = (
            grad
            - jnp.mean(grad, axis=-1, keepdims=True)
            - normed * jnp.mean(grad * normed, axis=-1, keepdims=True)
        ) * rstd
        g_hidden = dot(g_out.astype(BF16), w2[...], NT)
        dz_all[rows, :] = (g_hidden * (sigma + hidden * (1.0 - sigma))).astype(BF16)
    dz = dz_all[...]
    by_place = dot(scatter[...], dz).astype(BF16)
    summed[...] = by_place
    returned = dot(by_place[ROWS : ROWS + 2 * HALO], w1[WIDTH : 2 * WIDTH], NT).astype(BF16)
    theirs[SLOTS:, :] = returned[:HALO]
    ret_cross[...] = returned[HALO:]
    table = jnp.concatenate([nodes[...], halo], axis=0)
    weight[:WIDTH] = dot(edges_t[...], dz)
    weight[WIDTH : 2 * WIDTH] = dot(table, by_place[: ROWS + 2 * HALO], TN)
    weight[2 * WIDTH :] = dot(nodes[...], by_place[ROWS + 2 * HALO :], TN)
    for target, core in ((mine, odd), (theirs, 1 - odd)):
        for x, y in itertools.product(range(4), range(2)):
            pieces = []
            for quad in range(4):
                first = ((quad * 2 + y) * 4 + x) * 48 + core * 24
                pieces.append(weight[pl.ds(pl.multiple_of(first, 8), 24), :])
            place = (x * 2 + y) * 96
            target[place : place + 96, :] = jnp.concatenate(pieces, axis=0).astype(BF16)


def weight_terms(*args):
    shapes = (
        ((SLOTS, WIDTH), BF16),
        ((SLOTS + HALO, WIDTH), BF16),
        ((SLOTS, WIDTH), BF16),
        ((PLACES, WIDTH), BF16),
        ((HALO, WIDTH), BF16),
    )
    return pl.pallas_call(
        weight_kernel,
        out_shape=[pltpu.VMEM(s, d) for s, d in shapes],
        in_specs=[SMEM] + [VMEM] * 10,
        out_specs=[VMEM] * 5,
        scratch_shapes=[pltpu.VMEM((3 * WIDTH, WIDTH), F32)],
        compiler_params=pltpu.CompilerParams(vmem_limit_bytes=20 * 1024 * 1024),
        cost_estimate=pl.CostEstimate(
            flops=2_000_000_000, bytes_accessed=10_000_000, transcendentals=400_000
        ),
    )(*args)


def finish_kernel(grad_new, summed, dz, w1, d_edges, node_grad):
    node_grad[...] = dot(summed[:ROWS], w1[WIDTH : 2 * WIDTH], NT) + dot(
        summed[ROWS + 2 * HALO :], w1[2 * WIDTH :], NT
    )
    d_edges[...] = (grad_new[...] + dot(dz[...], w1[:WIDTH], NT)).astype(BF16)


def finish(*args):
    return pl.pallas_call(
        finish_kernel,
        out_shape=[
            jax.ShapeDtypeStruct((SLOTS, WIDTH), BF16),
            jax.ShapeDtypeStruct((ROWS, WIDTH), F32),
        ],
        in_specs=[VMEM] * 4,
        out_specs=[VMEM] * 2,
        compiler_params=pltpu.CompilerParams(vmem_limit_bytes=20 * 1024 * 1024),
        cost_estimate=pl.CostEstimate(
            flops=1_000_000_000, bytes_accessed=5_000_000, transcendentals=0
        ),
    )(*args)


def exchange(block, groups):
    return lax.all_to_all(block, AXES, 0, 0, axis_index_groups=groups)


def add_kernel(mine, other, result):
    result[...] = (mine[...].astype(F32) + other[:SLOTS].astype(F32)).astype(BF16)


def add(mine, other):
    return pl.pallas_call(
        add_kernel,
        out_shape=pltpu.VMEM((SLOTS, WIDTH), BF16),
        in_specs=[VMEM] * 2,
        out_specs=VMEM,
        compiler_params=pltpu.CompilerParams(vmem_limit_bytes=8 * 1024 * 1024),
    )(mine, other)


def sum_kernel(terms, result):
    values = jnp.sum(terms[...].astype(F32), axis=0).astype(result.dtype)
    if len(result.shape) == 2:
        result[...] = values
    else:
        for copy in range(result.shape[0]):
            result[copy] = values


def total(terms, dtype, copies=None):
    shape = terms.shape[1:] if copies is None else (copies,) + terms.shape[1:]
    return pl.pallas_call(
        sum_kernel,
        out_shape=pltpu.VMEM(shape, dtype) if dtype == BF16 else jax.ShapeDtypeStruct(shape, dtype),
        in_specs=[VMEM],
        out_specs=VMEM,
        compiler_params=pltpu.CompilerParams(vmem_limit_bytes=8 * 1024 * 1024),
    )(terms)


def per_device(
    nodes, edges, d_new_edges, d_aggregate, edge_w1, edge_w2, senders, receivers, edge_count
):
    here = lax.axis_index("patch")
    odd = here % 2
    first = nodes[:HALO]
    last = nodes[ROWS - HALO :]
    pair = lax.ppermute(jnp.where(odd == 0, last, first), "patch", PAIR)
    cross = lax.ppermute(jnp.where(odd == 0, first, last), "patch", CROSS)
    scalars = jnp.stack([here, odd, edge_count[0]]).astype(jnp.int32)
    base, grad_new, edges_t, scatter, halo_hot, w1, w2, own = prepare(
        scalars,
        senders.reshape(6, 128),
        receivers.reshape(6, 128),
        nodes,
        edges,
        d_new_edges,
        d_aggregate,
        edge_w1,
        edge_w2,
    )
    mine, theirs, dz, summed, ret_cross = weight_terms(
        scalars, pair, cross, base, grad_new, edges_t, scatter, halo_hot, w1, w2, own
    )
    other = lax.ppermute(theirs, "patch", PAIR)
    edge_grad, node_grad = finish(grad_new, summed, dz, w1)
    other, node_grad, ret_cross = lax.optimization_barrier((other, node_grad, ret_cross))
    from_pair = other[SLOTS:].astype(F32)
    from_cross = lax.ppermute(ret_cross, "patch", CROSS)
    weight = add(mine, other).reshape(8, 96, WIDTH)
    weight = total(exchange(weight, X_AND_Y_PAIR), BF16).reshape(4, 24, WIDTH)
    weight, from_cross = lax.optimization_barrier((weight, from_cross))
    from_cross = from_cross.astype(F32)
    weight = total(exchange(weight, Y_QUADS), BF16, 8)
    weight_grad = total(exchange(weight, Z_ALL), F32)
    from_lower = jnp.where(odd == 1, from_pair, from_cross)
    from_upper = jnp.where(odd == 1, from_cross, from_pair)
    gap = jnp.zeros((ROWS - 2 * HALO, WIDTH), F32)
    node_grad = node_grad + jnp.concatenate([from_lower, gap, from_upper], axis=0)
    return (node_grad.astype(BF16), edge_grad, weight_grad)


def solution(mesh):
    placed = (
        P(AXES, None),
        P(AXES, None),
        P(AXES, None),
        P(AXES, None),
        P(),
        P(),
        P(AXES),
        P(AXES),
        P(AXES),
    )
    return jax.shard_map(
        per_device,
        mesh=mesh,
        in_specs=placed,
        out_specs=(P(AXES, None), P(AXES, None), P("patch", None)),
        check_vma=False,
    )
```

time: 83.5 us -> 76.6 us (0.917)
  blocking collectives: 21.8 us -> 0 us
  waiting for transfers between devices: 15 us -> 26.2 us
  starting transfers between devices: 25.1 us -> 33.9 us
  local copies, waits for them, and re-layouts: 8.67 us -> 0.08 us
  Pallas kernels: 7.49 us -> 12.8 us
  other arithmetic: 3.28 us -> 1.62 us
    all_to_all x1 -> x0, blocking collectives: 21.8 us -> none  [exchange(): return lax.all_to_all(block, AXES, 0, 0, axis_index_groups=groups)]
    all_to_all x2 -> x3, waiting for transfers between devices: 12.1 us -> 25.8 us  [exchange(): return lax.all_to_all(block, AXES, 0, 0, axis_index_groups=groups)]
    all_to_all x2 -> x3, starting transfers between devices: 11.9 us -> 21.3 us  [exchange(): return lax.all_to_all(block, AXES, 0, 0, axis_index_groups=groups)]
    unnamed x16 -> x0, local copies, waits for them, and re-layouts: 7.9 us -> none
    pallas_call x1 -> x7, Pallas kernels: 7.49 us -> 12.8 us  [the longest x1 4.06 us: weight_terms(): pl.pallas_call(weight_kernel, out_shape=[pltpu.VMEM(s, d) for s, d in sha...]
    ppermute x1, waiting for transfers between devices: 2.25 us -> 0.48 us  [per_device(): other = lax.ppermute(theirs, 'patch', PAIR)]
    reduce_sum x3 -> x0, other arithmetic: 1.42 us -> none  [total(): return jnp.sum(block.astype(F32), axis=0)]
    ppermute x2 -> x1, starting transfers between devices: 5.39 us -> 4.06 us  [per_device(): from_cross = lax.ppermute(ret_cross, 'patch', CROSS)]
  transfers between devices with their start and end apart: 7 -> 7, of which waited for: 4 -> 4; matrix products, arithmetic and copies ran while one was open for 2% -> 1% of each run, Pallas kernels for 0% -> 8%
where the time goes in v2:
time: 76.6 us; the launch traced here: 76 us
  starting transfers between devices  33.9 us (44%)
  waiting for transfers between devices  26.2 us (34%)
  Pallas kernels  12.8 us (17%)
  other arithmetic  1.62 us (2%)
  between operations  1.37 us (2%)
    all_to_all x3, waiting for transfers between devices, exchange(): return lax.all_to_all(block, AXES, 0, 0, axis_index_groups=groups)  25.8 us
    all_to_all x3, starting transfers between devices, exchange(): return lax.all_to_all(block, AXES, 0, 0, axis_index_groups=groups)  21.3 us
    ppermute x1, starting transfers between devices, per_device(): cross = lax.ppermute(jnp.where(odd == 0, first, last), 'patch', CROSS)  4.66 us
    ppermute x1, starting transfers between devices, per_device(): from_cross = lax.ppermute(ret_cross, 'patch', CROSS)  4.06 us
    pallas_call x1, Pallas kernels, weight_terms(): pl.pallas_call(weight_kernel, out_shape=[pltpu.VMEM(s, d) for s, d in sha...  4.06 us
    pallas_call x1, Pallas kernels, prepare(): pl.pallas_call(prepare_kernel, out_shape=[pltpu.VMEM(s, d) for s, d in sh...  3.77 us
    pallas_call x3, Pallas kernels, total(): pl.pallas_call(sum_kernel, out_shape=pltpu.VMEM(shape, dtype) if dtype ==...  2.1 us
    ppermute x1, starting transfers between devices, per_device(): other = lax.ppermute(theirs, 'patch', PAIR)  1.92 us
  transfers between devices with their start and end apart: 7, of which 4 were waited for; matrix products, arithmetic and copies ran while one was open for 1% of the time, Pallas kernels for 8%

profile of v2, /device:TPU:8, one launch (start us, length us, event | category | flops | bytes accessed | tf_op | source)
XLA Modules:
  0.0 76.0 jit_solution(16742095896467265576)
XLA Ops:
  0.6 0.8 %broadcast_select_fusion = (bf16[32,512]{1,0:T(8,128)(2,1)S(1)}, bf16[32,512]{1,0:T(8,128)(2,1)S(1)}) fusion(pred[]{:T(512)S(6)} %eq.10, bf16[128,512]{1,0:T(8,128)(2,1)} %nodes_hbm.1), kind=kLoop, calls=%fused_computation.4 | loop fusion | flops 32768 | bytes 131073 | tf_op jit(solution)/shard_map/jit(_where)/select_n | solution.py:341
  1.4 1.9 %collective-permute-start = (bf16[32,512]{1,0:T(8,128)(2,1)S(1)}, bf16[32,512]{1,0:T(8,128)(2,1)S(1)}, u32[]{:S(2)}, u32[]{:S(2)}) collective-permute-start(bf16[32,512]{1,0:T(8,128)(2,1)S(1)} %get-tuple-element.46), channel_id=1, source_target_pairs={{0,8},{8,0},{16,24},{24,16},{32,40},{40,32},{48,56},{56,48},{64,72... | collective-permute-start | bytes 98312 | tf_op jit(solution)/shard_map/ppermute | solution.py:340
  3.3 4.7 %collective-permute-start.1 = (bf16[32,512]{1,0:T(8,128)(2,1)S(1)}, bf16[32,512]{1,0:T(8,128)(2,1)S(1)}, u32[]{:S(2)}, u32[]{:S(2)}) collective-permute-start(bf16[32,512]{1,0:T(8,128)(2,1)S(1)} %get-tuple-element.45), channel_id=1, source_target_pairs={{0,504},{8,16},{16,8},{24,32},{32,24},{40,48},{48,40},{56,64},{64,... | collective-permute-start | bytes 98312 | tf_op jit(solution)/shard_map/ppermute | solution.py:341
  8.7 0.1 pad_add_fusion.scalars
  8.7 3.8 %shard_map.112 = (f32[768,512]{1,0:T(8,128)S(1)}, f32[768,512]{1,0:T(8,128)S(1)}, bf16[512,768]{1,0:T(8,128)(2,1)S(1)}, bf16[320,768]{1,0:T(8,128)(2,1)S(1)}, bf...) custom-call(s32[3]{0:T(128)S(1)} %pad_add_fusion.scalars, ...), custom_call_target="tpu_custom_call" | custom-call | flops 2000000000 | bytes 10000000 | tf_op jit(solution)/shard_map/pallas_call | solution.py:172
  12.5 0.0 collective-permute-done.pair
  12.5 0.0 collective-permute-done.1.cross
  12.5 4.1 %shard_map.113 = (bf16[768,512]{1,0:T(8,128)(2,1)S(1)}, bf16[800,512]{1,0:T(8,128)(2,1)S(1)}, bf16[768,512]{1,0:T(8,128)(2,1)S(1)}, bf16[320,512]{1,0:T(8,128)(2,1)S(1)}, bf16[32,512]{1,0:T(8,128)(2,1)S(1)}) custom-call(s32[3]{0:T(128)S(1)} %pad_add_fusion.scalars, bf16[32,512]{1,0:T(8,128)(2,1)S(1)} %collective-permute-done.pair, ...), custom_call_target="tpu_custom_call" | custom-call | flops 2000000000 | bytes 10000000 | tf_op jit(solution)/shard_map/pallas_call | solution.py:259
  16.6 1.9 %collective-permute-start.2 = (bf16[800,512]{1,0:T(8,128)(2,1)S(1)}, bf16[800,512]{1,0:T(8,128)(2,1)S(1)}, u32[]{:S(2)}, u32[]{:S(2)}) collective-permute-start(bf16[800,512]{1,0:T(8,128)(2,1)S(1)} %get-tuple-element.31), channel_id=1, source_target_pairs={{0,8},{8,0},{16,24},{24,16},{32,40},{40,32},{48,56},{56,48},{64,72... | collective-permute-start | bytes 2457608 | tf_op jit(solution)/shard_map/ppermute | solution.py:357
  18.5 1.8 %shard_map.114 = (bf16[768,512]{1,0:T(8,128)(2,1)}, f32[128,512]{1,0:T(8,128)S(1)}) custom-call(f32[768,512]{1,0:T(8,128)S(1)} %get-tuple-element.24.grad_new, bf16[320,512]{1,0:T(8,128)(2,1)S(1)} %get-tuple-element.32.summed, bf16[768,512]{1,0:T(8,128)(2,1)S(1)} %get-tuple-element.33.dz, bf16[1536,512]{1,0:T(8,128)(2,1)S(1)} %get-tuple-element.28.w1), custom_call_target="tpu_custom_call" | custom-call | flops 1000000000 | bytes 5000000 | tf_op jit(solution)/shard_map/pallas_call | solution.py:280
  20.4 0.5 collective-permute-done.2.other
  20.8 1.1 %shard_map.115 = bf16[768,512]{1,0:T(8,128)(2,1)} custom-call(bf16[768,512]{1,0:T(8,128)(2,1)S(1)} %get-tuple-element.38.mine, bf16[800,512]{1,0:T(8,128)(2,1)S(1)} %collective-permute-done.2.other), custom_call_target="tpu_custom_call" | custom-call | tf_op jit(solution)/shard_map/pallas_call | solution.py:304
  21.9 8.6 %all-to-all-start = ((bf16[8,96,512]{2,1,0:T(8,128)(2,1)}), bf16[8,96,512]{2,1,0:T(8,128)(2,1)S(1)}, u32[]{:S(2)}, u32[]{:S(2)}) async-start(bf16[8,96,512]{2,1,0:T(8,128)(2,1)} %bitcast.4), calls=%async_computation | async-start | bytes 1572864 | tf_op jit(solution)/shard_map/all_to_all | solution.py:296
  30.6 4.1 %collective-permute-start.3 = (bf16[32,512]{1,0:T(8,128)(2,1)S(1)}, bf16[32,512]{1,0:T(8,128)(2,1)S(1)}, u32[]{:S(2)}, u32[]{:S(2)}) collective-permute-start(bf16[32,512]{1,0:T(8,128)(2,1)S(1)} %get-tuple-element.39), channel_id=1, source_target_pairs={{0,504},{8,16},{16,8},{24,32},{32,24},{40,48},{48,40},{56,64},{64,... | collective-permute-start | bytes 98312 | tf_op jit(solution)/shard_map/ppermute | solution.py:361
  34.6 8.6 %all-to-all-done.terms = bf16[8,96,512]{2,1,0:T(8,128)(2,1)S(1)} async-done(((bf16[8,96,512]{2,1,0:T(8,128)(2,1)}), bf16[8,96,512]{2,1,0:T(8,128)(2,1)S(1)}, u32[]{:S(2)}, u32[]{:S(2)}) %all-to-all-start) | async-done | bytes 786464 | tf_op jit(solution)/shard_map/all_to_all | solution.py:296
  43.2 0.7 shard_map.116
  44.0 0.0 collective-permute-done.3
  44.0 3.5 %all-to-all-start.1 = ((bf16[4,24,512]{2,1,0:T(8,128)(2,1)}), bf16[4,24,512]{2,1,0:T(8,128)(2,1)S(1)}, u32[]{:S(2)}, u32[]{:S(2)}) async-start(bf16[4,24,512]{2,1,0:T(8,128)(2,1)} %bitcast.5), calls=%async_computation.1 | async-start | bytes 196608 | tf_op jit(solution)/shard_map/all_to_all | solution.py:296
  47.5 0.1 pad.1.clone
  47.5 8.1 %all-to-all-done.1.terms = bf16[4,24,512]{2,1,0:T(8,128)(2,1)S(1)} async-done(((bf16[4,24,512]{2,1,0:T(8,128)(2,1)}), bf16[4,24,512]{2,1,0:T(8,128)(2,1)S(1)}, u32[]{:S(2)}, u32[]{:S(2)}) %all-to-all-start.1) | async-done | bytes 98336 | tf_op jit(solution)/shard_map/all_to_all | solution.py:296
  55.7 0.7 shard_map.117
  56.4 9.2 %all-to-all-start.2 = ((bf16[8,24,512]{2,1,0:T(8,128)(2,1)}), bf16[8,24,512]{2,1,0:T(8,128)(2,1)S(1)}, u32[]{:S(2)}, u32[]{:S(2)}) async-start(bf16[8,24,512]{2,1,0:T(8,128)(2,1)} %shard_map.117), calls=%async_computation.2 | async-start | bytes 393216 | tf_op jit(solution)/shard_map/all_to_all | solution.py:296
  65.6 0.7 fusion
  66.3 9.0 %all-to-all-done.2.terms = bf16[8,24,512]{2,1,0:T(8,128)(2,1)S(1)} async-done(((bf16[8,24,512]{2,1,0:T(8,128)(2,1)}), bf16[8,24,512]{2,1,0:T(8,128)(2,1)S(1)}, u32[]{:S(2)}, u32[]{:S(2)}) %all-to-all-start.2) | async-done | bytes 196640 | tf_op jit(solution)/shard_map/all_to_all | solution.py:296
  75.4 0.6 shard_map.118
  (2 shorter events, 0.0 us)
Async XLA Ops:
  1.4 11.1 %collective-permute-start = (bf16[32,512]{1,0:T(8,128)(2,1)S(1)}, bf16[32,512]{1,0:T(8,128)(2,1)S(1)}, u32[]{:S(2)}, u32[]{:S(2)}) collective-permute-start(bf16[32,512]{1,0:T(8,128)(2,1)S(1)} %get-tuple-element.46), channel_id=1, source_target_pairs={{0,8},{8,0},{16,24},{24,16},{32,40},{40,32},{48,56},{56,48},{64,72... | collective-permute-start | bytes 98312 | tf_op jit(solution)/shard_map/ppermute | solution.py:340
  3.3 9.2 %collective-permute-start.1 = (bf16[32,512]{1,0:T(8,128)(2,1)S(1)}, bf16[32,512]{1,0:T(8,128)(2,1)S(1)}, u32[]{:S(2)}, u32[]{:S(2)}) collective-permute-start(bf16[32,512]{1,0:T(8,128)(2,1)S(1)} %get-tuple-element.45), channel_id=1, source_target_pairs={{0,504},{8,16},{16,8},{24,32},{32,24},{40,48},{48,40},{56,64},{64,... | collective-permute-start | bytes 98312 | tf_op jit(solution)/shard_map/ppermute | solution.py:341
  16.6 4.2 %collective-permute-start.2 = (bf16[800,512]{1,0:T(8,128)(2,1)S(1)}, bf16[800,512]{1,0:T(8,128)(2,1)S(1)}, u32[]{:S(2)}, u32[]{:S(2)}) collective-permute-start(bf16[800,512]{1,0:T(8,128)(2,1)S(1)} %get-tuple-element.31), channel_id=1, source_target_pairs={{0,8},{8,0},{16,24},{24,16},{32,40},{40,32},{48,56},{56,48},{64,72... | collective-permute-start | bytes 2457608 | tf_op jit(solution)/shard_map/ppermute | solution.py:357
  21.9 21.3 %all-to-all-start = ((bf16[8,96,512]{2,1,0:T(8,128)(2,1)}), bf16[8,96,512]{2,1,0:T(8,128)(2,1)S(1)}, u32[]{:S(2)}, u32[]{:S(2)}) async-start(bf16[8,96,512]{2,1,0:T(8,128)(2,1)} %bitcast.4), calls=%async_computation | async-start | bytes 1572864 | tf_op jit(solution)/shard_map/all_to_all | solution.py:296
  30.6 13.4 %collective-permute-start.3 = (bf16[32,512]{1,0:T(8,128)(2,1)S(1)}, bf16[32,512]{1,0:T(8,128)(2,1)S(1)}, u32[]{:S(2)}, u32[]{:S(2)}) collective-permute-start(bf16[32,512]{1,0:T(8,128)(2,1)S(1)} %get-tuple-element.39), channel_id=1, source_target_pairs={{0,504},{8,16},{16,8},{24,32},{32,24},{40,48},{48,40},{56,64},{64,... | collective-permute-start | bytes 98312 | tf_op jit(solution)/shard_map/ppermute | solution.py:361
  44.0 11.7 %all-to-all-start.1 = ((bf16[4,24,512]{2,1,0:T(8,128)(2,1)}), bf16[4,24,512]{2,1,0:T(8,128)(2,1)S(1)}, u32[]{:S(2)}, u32[]{:S(2)}) async-start(bf16[4,24,512]{2,1,0:T(8,128)(2,1)} %bitcast.5), calls=%async_computation.1 | async-start | bytes 196608 | tf_op jit(solution)/shard_map/all_to_all | solution.py:296
  56.4 19.0 %all-to-all-start.2 = ((bf16[8,24,512]{2,1,0:T(8,128)(2,1)}), bf16[8,24,512]{2,1,0:T(8,128)(2,1)S(1)}, u32[]{:S(2)}, u32[]{:S(2)}) async-start(bf16[8,24,512]{2,1,0:T(8,128)(2,1)} %shard_map.117), calls=%async_computation.2 | async-start | bytes 393216 | tf_op jit(solution)/shard_map/all_to_all | solution.py:296

commit v3 on v2

--- a/solution.py
+++ b/solution.py
@@ -12,6 +12,7 @@
 SLOTS = 768
 WIDTH = 512
 PLACES = 2 * ROWS + 2 * HALO
+HALF = WIDTH // 2
 BLOCK = 768
 AXES = ("patch", "band")
 BF16 = jnp.bfloat16
@@ -30,10 +31,9 @@
     return groups
 
 
-SINGLE_X, SINGLE_Y, SINGLE_Z = ([[i] for i in range(n)] for n in (4, 8, 8))
-X_AND_Y_PAIR = device_groups([[2 * i, 2 * i + 1] for i in range(4)], [list(range(4))], SINGLE_Z)
-Y_QUADS = device_groups([[0, 2, 4, 6], [1, 3, 5, 7]], SINGLE_X, SINGLE_Z)
-Z_ALL = device_groups(SINGLE_Y, SINGLE_X, [list(range(8))])
+PAIRS_OF_8 = [[2 * i, 2 * i + 1] for i in range(4)]
+NEAR = device_groups(PAIRS_OF_8, [list(range(4))], PAIRS_OF_8)
+FAR = device_groups([[0, 2, 4, 6], [1, 3, 5, 7]], [[i] for i in range(4)], [list(range(8))])
 PAIR = [(i, i ^ 1) for i in range(64)]
 CROSS = [(i, (i - 1) % 64 if i % 2 == 0 else (i + 1) % 64) for i in range(64)]
 
@@ -56,7 +56,7 @@
 
 
 def prepare_kernel(
-    scalars,
+    count,
     senders_hbm,
     receivers_hbm,
     nodes_hbm,
@@ -93,7 +93,8 @@
     copies = [pltpu.make_async_copy(a, b, sems.at[i]) for i, (a, b) in enumerate(pairs)]
     for copy in copies:
         copy.start()
-    here, odd, count = scalars[0], scalars[1], scalars[2]
+    here = lax.axis_index("patch")
+    odd = here % 2
     copies[0].wait()
     copies[1].wait()
     owner = senders[...] // (ROWS * 8)
@@ -147,11 +148,12 @@
         edges_t[:, rows] = edges[rows, :].T
     copies[5].wait()
     copies[6].wait()
+    limit = jnp.broadcast_to(count[0:1, 0:1], (SLOTS, 1))
     for start in range(0, SLOTS, BLOCK):
         rows = slice(start, start + BLOCK)
         parts = range(start // 128, (start + BLOCK) // 128)
         slot = start + lax.broadcasted_iota(jnp.int32, (BLOCK, 1), 0)
-        live = jnp.where(slot < count, 1.0, 0.0)
+        live = jnp.where(slot < limit[rows], 1.0, 0.0)
         taken = dot(jnp.concatenate([recv_hot[p] for p in parts], axis=0), d_agg[...])
         grad_new[rows, :] = live * (d_new[rows, :].astype(F32) + taken)
     copies[7].wait()
@@ -172,7 +174,7 @@
     return pl.pallas_call(
         prepare_kernel,
         out_shape=[pltpu.VMEM(s, d) for s, d in shapes],
-        in_specs=[SMEM] + [HBM] * 8,
+        in_specs=[VMEM] + [HBM] * 8,
         out_specs=[VMEM] * 8,
         scratch_shapes=[
             pltpu.VMEM((SLOTS, WIDTH), BF16),
@@ -190,9 +192,8 @@
 
 
 def weight_kernel(
-    scalars,
+    cross,
     pair,
-    cross,
     base,
     grad_new,
     edges_t,
@@ -208,8 +209,10 @@
     ret_cross,
     weight,
 ):
-    odd = scalars[1]
-    halo = jnp.concatenate([pair[...], cross[...]], axis=0)
+    odd = lax.axis_index("patch") % 2
+    first = pl.multiple_of(odd * (ROWS - HALO), HALO)
+    last = pl.multiple_of((1 - odd) * (ROWS - HALO), HALO)
+    halo = jnp.concatenate([pair[pl.ds(first, HALO), :], cross[pl.ds(last, HALO), :]], axis=0)
     halo_product = halves(dot(halo, w1[WIDTH : 2 * WIDTH]))
     for start in range(0, SLOTS, BLOCK):
         rows = slice(start, start + BLOCK)
@@ -232,26 +235,28 @@
     by_place = dot(scatter[...], dz).astype(BF16)
     summed[...] = by_place
     returned = dot(by_place[ROWS : ROWS + 2 * HALO], w1[WIDTH : 2 * WIDTH], NT).astype(BF16)
-    theirs[SLOTS:, :] = returned[:HALO]
+    theirs[2 * SLOTS : 2 * SLOTS + HALO, :] = returned[:HALO, :HALF]
+    theirs[2 * SLOTS + HALO :, :] = returned[:HALO, HALF:]
     ret_cross[...] = returned[HALO:]
     table = jnp.concatenate([nodes[...], halo], axis=0)
     weight[:WIDTH] = dot(edges_t[...], dz)
     weight[WIDTH : 2 * WIDTH] = dot(table, by_place[: ROWS + 2 * HALO], TN)
     weight[2 * WIDTH :] = dot(nodes[...], by_place[ROWS + 2 * HALO :], TN)
     for target, core in ((mine, odd), (theirs, 1 - odd)):
-        for x, y in itertools.product(range(4), range(2)):
+        for x, y, z in itertools.product(range(4), range(2), range(2)):
             pieces = []
             for quad in range(4):
                 first = ((quad * 2 + y) * 4 + x) * 48 + core * 24
-                pieces.append(weight[pl.ds(pl.multiple_of(first, 8), 24), :])
-            place = (x * 2 + y) * 96
+                rows = pl.ds(pl.multiple_of(first, 8), 24)
+                pieces.append(weight[rows, z * HALF : z * HALF + HALF])
+            place = ((x * 2 + y) * 2 + z) * 96
             target[place : place + 96, :] = jnp.concatenate(pieces, axis=0).astype(BF16)
 
 
 def weight_terms(*args):
     shapes = (
-        ((SLOTS, WIDTH), BF16),
-        ((SLOTS + HALO, WIDTH), BF16),
+        ((2 * SLOTS, HALF), BF16),
+        ((2 * SLOTS + 2 * HALO, HALF), BF16),
         ((SLOTS, WIDTH), BF16),
         ((PLACES, WIDTH), BF16),
         ((HALO, WIDTH), BF16),
@@ -259,7 +264,7 @@
     return pl.pallas_call(
         weight_kernel,
         out_shape=[pltpu.VMEM(s, d) for s, d in shapes],
-        in_specs=[SMEM] + [VMEM] * 10,
+        in_specs=[VMEM] * 10,
         out_specs=[VMEM] * 5,
         scratch_shapes=[pltpu.VMEM((3 * WIDTH, WIDTH), F32)],
         compiler_params=pltpu.CompilerParams(vmem_limit_bytes=20 * 1024 * 1024),
@@ -296,38 +301,34 @@
     return lax.all_to_all(block, AXES, 0, 0, axis_index_groups=groups)
 
 
-def add_kernel(mine, other, result):
-    result[...] = (mine[...].astype(F32) + other[:SLOTS].astype(F32)).astype(BF16)
-
-
-def add(mine, other):
+def small_call(body, shape, dtype, *args):
     return pl.pallas_call(
-        add_kernel,
-        out_shape=pltpu.VMEM((SLOTS, WIDTH), BF16),
-        in_specs=[VMEM] * 2,
+        body,
+        out_shape=pltpu.VMEM(shape, dtype) if dtype == BF16 else jax.ShapeDtypeStruct(shape, dtype),
+        in_specs=[VMEM] * len(args),
         out_specs=VMEM,
         compiler_params=pltpu.CompilerParams(vmem_limit_bytes=8 * 1024 * 1024),
-    )(mine, other)
-
-
-def sum_kernel(terms, result):
-    values = jnp.sum(terms[...].astype(F32), axis=0).astype(result.dtype)
-    if len(result.shape) == 2:
-        result[...] = values
-    else:
-        for copy in range(result.shape[0]):
-            result[copy] = values
-
-
-def total(terms, dtype, copies=None):
-    shape = terms.shape[1:] if copies is None else (copies,) + terms.shape[1:]
-    return pl.pallas_call(
-        sum_kernel,
-        out_shape=pltpu.VMEM(shape, dtype) if dtype == BF16 else jax.ShapeDtypeStruct(shape, dtype),
-        in_specs=[VMEM],
-        out_specs=VMEM,
-        compiler_params=pltpu.CompilerParams(vmem_limit_bytes=8 * 1024 * 1024),
-    )(terms)
+    )(*args)
+
+
+def add_kernel(mine, other, result):
+    result[...] = (mine[...].astype(F32) + other[: 2 * SLOTS].astype(F32)).astype(BF16)
+
+
+def near_kernel(terms, result):
+    values = jnp.sum(terms[...].astype(F32), axis=0)
+    for quad in range(4):
+        piece = values[quad * 24 : quad * 24 + 24].astype(BF16)
+        for z in range(8):
+            result[quad * 8 + z] = piece
+
+
+def far_kernel(terms, result):
+    for half in range(2):
+        values = terms[half].astype(F32)
+        for place in range(2 + half, 32, 2):
+            values = values + terms[place].astype(F32)
+        result[:, half * HALF : half * HALF + HALF] = values
 
 
 def per_device(
@@ -335,13 +336,10 @@
 ):
     here = lax.axis_index("patch")
     odd = here % 2
-    first = nodes[:HALO]
-    last = nodes[ROWS - HALO :]
-    pair = lax.ppermute(jnp.where(odd == 0, last, first), "patch", PAIR)
-    cross = lax.ppermute(jnp.where(odd == 0, first, last), "patch", CROSS)
-    scalars = jnp.stack([here, odd, edge_count[0]]).astype(jnp.int32)
+    cross = lax.ppermute(nodes, "patch", CROSS)
+    pair = lax.ppermute(nodes, "patch", PAIR)
     base, grad_new, edges_t, scatter, halo_hot, w1, w2, own = prepare(
-        scalars,
+        jnp.broadcast_to(edge_count, (8, 128)),
         senders.reshape(6, 128),
         receivers.reshape(6, 128),
         nodes,
@@ -352,19 +350,18 @@
         edge_w2,
     )
     mine, theirs, dz, summed, ret_cross = weight_terms(
-        scalars, pair, cross, base, grad_new, edges_t, scatter, halo_hot, w1, w2, own
+        cross, pair, base, grad_new, edges_t, scatter, halo_hot, w1, w2, own
     )
     other = lax.ppermute(theirs, "patch", PAIR)
     edge_grad, node_grad = finish(grad_new, summed, dz, w1)
-    other, node_grad, ret_cross = lax.optimization_barrier((other, node_grad, ret_cross))
-    from_pair = other[SLOTS:].astype(F32)
-    from_cross = lax.ppermute(ret_cross, "patch", CROSS)
-    weight = add(mine, other).reshape(8, 96, WIDTH)
-    weight = total(exchange(weight, X_AND_Y_PAIR), BF16).reshape(4, 24, WIDTH)
-    weight, from_cross = lax.optimization_barrier((weight, from_cross))
-    from_cross = from_cross.astype(F32)
-    weight = total(exchange(weight, Y_QUADS), BF16, 8)
-    weight_grad = total(exchange(weight, Z_ALL), F32)
+    other, node_grad = lax.optimization_barrier((other, node_grad))
+    from_pair = jnp.concatenate([other[2 * SLOTS : -HALO], other[-HALO:]], axis=1).astype(F32)
+    weight = small_call(add_kernel, (2 * SLOTS, HALF), BF16, mine, other)
+    weight = exchange(weight.reshape(16, 96, HALF), NEAR)
+    weight = small_call(near_kernel, (32, 24, HALF), BF16, weight)
+    weight, ret_cross = lax.optimization_barrier((weight, ret_cross))
+    from_cross = lax.ppermute(ret_cross, "patch", CROSS).astype(F32)
+    weight_grad = small_call(far_kernel, (24, WIDTH), F32, exchange(weight, FAR))
     from_lower = jnp.where(odd == 1, from_pair, from_cross)
     from_upper = jnp.where(odd == 1, from_cross, from_pair)
     gap = jnp.zeros((ROWS - 2 * HALO, WIDTH), F32)

time: 76.6 us -> 69.9 us (0.913)
  blocking collectives: 0 us -> 21.1 us
  waiting for transfers between devices: 26.2 us -> 13.4 us
  starting transfers between devices: 33.9 us -> 22.4 us
  Pallas kernels: 12.8 us -> 10.4 us
  other arithmetic: 1.62 us -> 0.76 us
    all_to_all x0 -> x1, blocking collectives: none -> 21.1 us  [exchange(): return lax.all_to_all(block, AXES, 0, 0, axis_index_groups=groups)]
    all_to_all x3 -> x1, waiting for transfers between devices: 25.8 us -> 6.12 us  [exchange(): return lax.all_to_all(block, AXES, 0, 0, axis_index_groups=groups)]
    all_to_all x3 -> x1, starting transfers between devices: 21.3 us -> 12.2 us  [exchange(): return lax.all_to_all(block, AXES, 0, 0, axis_index_groups=groups)]
    ppermute x3, waiting for transfers between devices: 0.01 us -> 7.18 us  [the longest x1 7.18 us: per_device(): from_cross = lax.ppermute(ret_cross, 'patch', CROSS).astype(F32)]
    ppermute x3, starting transfers between devices: 10.6 us -> 7.83 us  [the longest x1 3.99 us: per_device(): cross = lax.ppermute(nodes, 'patch', CROSS)]
    pallas_call x4 -> x3, Pallas kernels: 3.19 us -> 1.72 us  [small_call(): pl.pallas_call(body, out_shape=pltpu.VMEM(shape, dtype) if dtype == BF16...]
    select_n x1 -> x0, other arithmetic: 0.79 us -> none  [per_device(): cross = lax.ppermute(jnp.where(odd == 0, first, last), 'patch', CROSS)]
  transfers between devices with their start and end apart: 7 -> 5, of which waited for: 4 -> 3; matrix products, arithmetic and copies ran while one was open for 1% -> 1% of each run, Pallas kernels for 8% -> 7%
where the time goes in v3:
time: 69.9 us; the launch traced here: 69.6 us
  starting transfers between devices  22.4 us (32%)
  blocking collectives  21.1 us (30%)
  waiting for transfers between devices  13.4 us (19%)
  Pallas kernels  10.4 us (15%)
  between operations  1.39 us (2%)
  other arithmetic  0.76 us (1%)
    all_to_all x1, blocking collectives, exchange(): return lax.all_to_all(block, AXES, 0, 0, axis_index_groups=groups)  21.1 us
    all_to_all x1, starting transfers between devices, exchange(): return lax.all_to_all(block, AXES, 0, 0, axis_index_groups=groups)  12.2 us
    ppermute x1, waiting for transfers between devices, per_device(): from_cross = lax.ppermute(ret_cross, 'patch', CROSS).astype(F32)  7.18 us
    all_to_all x1, waiting for transfers between devices, exchange(): return lax.all_to_all(block, AXES, 0, 0, axis_index_groups=groups)  6.12 us
    ppermute x1, starting transfers between devices, per_device(): cross = lax.ppermute(nodes, 'patch', CROSS)  3.99 us
    pallas_call x1, Pallas kernels, weight_terms(): pl.pallas_call(weight_kernel, out_shape=[pltpu.VMEM(s, d) for s, d in sha...  3.61 us
    pallas_call x1, Pallas kernels, prepare(): pl.pallas_call(prepare_kernel, out_shape=[pltpu.VMEM(s, d) for s, d in sh...  3.24 us
    ppermute x1, starting transfers between devices, per_device(): other = lax.ppermute(theirs, 'patch', PAIR)  2.4 us
  transfers between devices with their start and end apart: 5, of which 3 were waited for; matrix products, arithmetic and copies ran while one was open for 1% of the time, Pallas kernels for 7%

profile of v3, /device:TPU:8, one launch (start us, length us, event | category | flops | bytes accessed | tf_op | source)
XLA Modules:
  0.0 69.6 jit_solution(2510426518865127873)
XLA Ops:
  0.6 4.0 %collective-permute-start = (bf16[128,512]{1,0:T(8,128)(2,1)}, bf16[128,512]{1,0:T(8,128)(2,1)S(1)}, u32[]{:S(2)}, u32[]{:S(2)}) collective-permute-start(bf16[128,512]{1,0:T(8,128)(2,1)} %nodes_hbm.1), channel_id=1, source_target_pairs={{0,504},{8,16},{16,8},{24,32},{32,24},{40,48},{48,40},{56,64},{64,... | collective-permute-start | bytes 393224 | tf_op jit(solution)/shard_map/ppermute | solution.py:339
  4.6 1.9 %collective-permute-start.1 = (bf16[128,512]{1,0:T(8,128)(2,1)}, bf16[128,512]{1,0:T(8,128)(2,1)S(1)}, u32[]{:S(2)}, u32[]{:S(2)}) collective-permute-start(bf16[128,512]{1,0:T(8,128)(2,1)} %nodes_hbm.1), channel_id=1, source_target_pairs={{0,8},{8,0},{16,24},{24,16},{32,40},{40,32},{48,56},{56,48},{64,72... | collective-permute-start | bytes 393224 | tf_op jit(solution)/shard_map/ppermute | solution.py:340
  7.2 3.2 %shard_map.115 = (f32[768,512]{1,0:T(8,128)S(1)}, f32[768,512]{1,0:T(8,128)S(1)}, bf16[512,768]{1,0:T(8,128)(2,1)S(1)}, bf16[320,768]{1,0:T(8,128)(2,1)S(1)}, bf...) custom-call(s32[8,128]{1,0:T(8,128)S(1)} %broadcast_in_dim.8.count, ...), custom_call_target="tpu_custom_call" | custom-call | flops 2000000000 | bytes 10000000 | tf_op jit(solution)/shard_map/pallas_call | solution.py:174
  10.5 0.0 collective-permute-done.cross
  10.5 0.0 collective-permute-done.1.pair
  10.5 3.6 %shard_map.116 = (bf16[1536,256]{1,0:T(8,128)(2,1)S(1)}, bf16[1600,256]{1,0:T(8,128)(2,1)S(1)}, bf16[768,512]{1,0:T(8,128)(2,1)S(1)}, bf16[320,512]{1,0:T(8,128)(2,1)S(1)}, bf16[32,512]{1,0:T(8,128)(2,1)S(1)}) custom-call(bf16[128,512]{1,0:T(8,128)(2,1)S(1)} %collective-permute-done.cross, bf16[128,512]{1,0:T(8,128)(2,1)S(1)} %collective-permute-done.1.pair, ...), custom_call_target="tpu_custom_call" | custom-call | flops 2000000000 | bytes 10000000 | tf_op jit(solution)/shard_map/pallas_call | solution.py:264
  14.1 2.4 %collective-permute-start.2 = (bf16[1600,256]{1,0:T(8,128)(2,1)S(1)}, bf16[1600,256]{1,0:T(8,128)(2,1)S(1)}, u32[]{:S(2)}, u32[]{:S(2)}) collective-permute-start(bf16[1600,256]{1,0:T(8,128)(2,1)S(1)} %get-tuple-element.30), channel_id=1, source_target_pairs={{0,8},{8,0},{16,24},{24,16},{32,40},{40,32},{48,56},{56,48},{64,72... | collective-permute-start | bytes 2457608 | tf_op jit(solution)/shard_map/ppermute | solution.py:355
  16.5 1.8 %shard_map.117 = (bf16[768,512]{1,0:T(8,128)(2,1)}, f32[128,512]{1,0:T(8,128)S(1)}) custom-call(f32[768,512]{1,0:T(8,128)S(1)} %get-tuple-element.23.grad_new, bf16[320,512]{1,0:T(8,128)(2,1)S(1)} %get-tuple-element.31.summed, bf16[768,512]{1,0:T(8,128)(2,1)S(1)} %get-tuple-element.32.dz, bf16[1536,512]{1,0:T(8,128)(2,1)S(1)} %get-tuple-element.27.w1), custom_call_target="tpu_custom_call" | custom-call | flops 1000000000 | bytes 5000000 | tf_op jit(solution)/shard_map/pallas_call | solution.py:285
  18.3 0.1 collective-permute-done.2.other
  18.4 0.2 shard_map.118
  18.6 21.1 %all_to_all.10.terms = bf16[16,96,256]{2,1,0:T(8,128)(2,1)S(1)} all-to-all(bf16[16,96,256]{2,1,0:T(8,128)(2,1)S(1)} %bitcast.5), channel_id=1, replica_groups={{0,1,64,65,16,17,80,81,32,33,96,97,48,49,112,113},{8,9,72,73,24,25,88,8..., dimensions={0} | all-to-all | bytes 1572864 | tf_op jit(solution)/shard_map/all_to_all | solution.py:301
  39.7 0.9 %shard_map.119 = bf16[32,24,256]{2,1,0:T(8,128)(2,1)} custom-call(bf16[16,96,256]{2,1,0:T(8,128)(2,1)S(1)} %all_to_all.10.terms), custom_call_target="tpu_custom_call" | custom-call | tf_op jit(solution)/shard_map/pallas_call | solution.py:305
  40.6 12.2 %all-to-all-start.1 = ((bf16[32,24,256]{2,1,0:T(8,128)(2,1)}), bf16[32,24,256]{2,1,0:T(8,128)(2,1)S(1)}, u32[]{:S(2)}, u32[]{:S(2)}) async-start(bf16[32,24,256]{2,1,0:T(8,128)(2,1)} %shard_map.119), calls=%async_computation.1 | async-start | bytes 786432 | tf_op jit(solution)/shard_map/all_to_all | solution.py:301
  52.8 0.1 pad.1.clone
  52.9 1.9 %collective-permute-start.3 = (bf16[32,512]{1,0:T(8,128)(2,1)S(1)}, bf16[32,512]{1,0:T(8,128)(2,1)S(1)}, u32[]{:S(2)}, u32[]{:S(2)}) collective-permute-start(bf16[32,512]{1,0:T(8,128)(2,1)S(1)} %get-tuple-element.38), channel_id=1, source_target_pairs={{0,504},{8,16},{16,8},{24,32},{32,24},{40,48},{48,40},{56,64},{64,... | collective-permute-start | bytes 98312 | tf_op jit(solution)/shard_map/ppermute | solution.py:363
  54.8 7.2 %collective-permute-done.3 = bf16[32,512]{1,0:T(8,128)(2,1)S(1)} collective-permute-done((bf16[32,512]{1,0:T(8,128)(2,1)S(1)}, bf16[32,512]{1,0:T(8,128)(2,1)S(1)}, u32[]{:S(2)}, u32[]{:S(2)}) %collective-permute-start.3) | collective-permute-done | bytes 32800 | tf_op jit(solution)/shard_map/ppermute | solution.py:363
  62.0 0.7 %fusion = bf16[128,512]{1,0:T(8,128)(2,1)} fusion(f32[128,512]{1,0:T(8,128)S(1)} %get-tuple-element.34, f32[32,512]{1,0:T(8,128)S(1)} %get-tuple-element.44, f32[32,512]{1,0:T(8,128)S(1)} %get-tuple-element.43, f32[128]{0:T(128)S(1)} %pad.1.clone), kind=kLoop, calls=%fused_computation.1 | loop fusion | flops 262144 | bytes 524800 | tf_op jit(solution)/shard_map/convert_element_type | solution.py:369
  62.8 6.1 %all-to-all-done.1.terms = bf16[32,24,256]{2,1,0:T(8,128)(2,1)S(1)} async-done(((bf16[32,24,256]{2,1,0:T(8,128)(2,1)}), bf16[32,24,256]{2,1,0:T(8,128)(2,1)S(1)}, u32[]{:S(2)}, u32[]{:S(2)}) %all-to-all-start.1) | async-done | bytes 393248 | tf_op jit(solution)/shard_map/all_to_all | solution.py:301
  68.9 0.7 shard_map.120
  (4 shorter events, 0.0 us)
Async XLA Ops:
  0.6 9.8 %collective-permute-start = (bf16[128,512]{1,0:T(8,128)(2,1)}, bf16[128,512]{1,0:T(8,128)(2,1)S(1)}, u32[]{:S(2)}, u32[]{:S(2)}) collective-permute-start(bf16[128,512]{1,0:T(8,128)(2,1)} %nodes_hbm.1), channel_id=1, source_target_pairs={{0,504},{8,16},{16,8},{24,32},{32,24},{40,48},{48,40},{56,64},{64,... | collective-permute-start | bytes 393224 | tf_op jit(solution)/shard_map/ppermute | solution.py:339
  4.6 5.8 %collective-permute-start.1 = (bf16[128,512]{1,0:T(8,128)(2,1)}, bf16[128,512]{1,0:T(8,128)(2,1)S(1)}, u32[]{:S(2)}, u32[]{:S(2)}) collective-permute-start(bf16[128,512]{1,0:T(8,128)(2,1)} %nodes_hbm.1), channel_id=1, source_target_pairs={{0,8},{8,0},{16,24},{24,16},{32,40},{40,32},{48,56},{56,48},{64,72... | collective-permute-start | bytes 393224 | tf_op jit(solution)/shard_map/ppermute | solution.py:340
  14.1 4.3 %collective-permute-start.2 = (bf16[1600,256]{1,0:T(8,128)(2,1)S(1)}, bf16[1600,256]{1,0:T(8,128)(2,1)S(1)}, u32[]{:S(2)}, u32[]{:S(2)}) collective-permute-start(bf16[1600,256]{1,0:T(8,128)(2,1)S(1)} %get-tuple-element.30), channel_id=1, source_target_pairs={{0,8},{8,0},{16,24},{24,16},{32,40},{40,32},{48,56},{56,48},{64,72... | collective-permute-start | bytes 2457608 | tf_op jit(solution)/shard_map/ppermute | solution.py:355
  40.6 28.3 %all-to-all-start.1 = ((bf16[32,24,256]{2,1,0:T(8,128)(2,1)}), bf16[32,24,256]{2,1,0:T(8,128)(2,1)S(1)}, u32[]{:S(2)}, u32[]{:S(2)}) async-start(bf16[32,24,256]{2,1,0:T(8,128)(2,1)} %shard_map.119), calls=%async_computation.1 | async-start | bytes 786432 | tf_op jit(solution)/shard_map/all_to_all | solution.py:301
  52.9 9.1 %collective-permute-start.3 = (bf16[32,512]{1,0:T(8,128)(2,1)S(1)}, bf16[32,512]{1,0:T(8,128)(2,1)S(1)}, u32[]{:S(2)}, u32[]{:S(2)}) collective-permute-start(bf16[32,512]{1,0:T(8,128)(2,1)S(1)} %get-tuple-element.38), channel_id=1, source_target_pairs={{0,504},{8,16},{16,8},{24,32},{32,24},{40,48},{48,40},{56,64},{64,... | collective-permute-start | bytes 98312 | tf_op jit(solution)/shard_map/ppermute | solution.py:363

commit v4 on v3

--- a/solution.py
+++ b/solution.py
@@ -31,9 +31,14 @@
     return groups
 
 
-PAIRS_OF_8 = [[2 * i, 2 * i + 1] for i in range(4)]
+PAIR_ORDER = (1, 0)
+QUAD_ORDER = (1, 2, 3, 0)
+Z_ORDER = (7, 6, 5, 4, 3, 2, 1, 0)
+PAIRS_OF_8 = [[2 * i + k for k in PAIR_ORDER] for i in range(4)]
 NEAR = device_groups(PAIRS_OF_8, [list(range(4))], PAIRS_OF_8)
-FAR = device_groups([[0, 2, 4, 6], [1, 3, 5, 7]], [[i] for i in range(4)], [list(range(8))])
+FAR = device_groups(
+    [[2 * q + k for q in QUAD_ORDER] for k in range(2)], [[i] for i in range(4)], [Z_ORDER]
+)
 PAIR = [(i, i ^ 1) for i in range(64)]
 CROSS = [(i, (i - 1) % 64 if i % 2 == 0 else (i + 1) % 64) for i in range(64)]
 
@@ -55,48 +60,41 @@
     return jnp.concatenate([high, (values - high.astype(F32)).astype(BF16)], axis=0)
 
 
+def lane_kernel(after, lane):
+    lane[...] = lax.broadcasted_iota(jnp.int32, (128, 128), 1)
+
+
+def lane_index(after):
+    return pl.pallas_call(
+        lane_kernel,
+        out_shape=pltpu.VMEM((128, 128), jnp.int32),
+        in_specs=[HBM],
+        out_specs=VMEM,
+        compiler_params=pltpu.CompilerParams(vmem_limit_bytes=8 * 1024 * 1024),
+        cost_estimate=pl.CostEstimate(
+            flops=20_000_000_000, bytes_accessed=100_000, transcendentals=0
+        ),
+    )(after)
+
+
 def prepare_kernel(
     count,
-    senders_hbm,
-    receivers_hbm,
-    nodes_hbm,
-    edges_hbm,
-    d_new_hbm,
-    d_agg_hbm,
-    w1_hbm,
-    w2_hbm,
+    senders,
+    receivers,
+    lane_ref,
+    nodes,
+    edges,
+    d_new,
+    d_agg,
+    w1,
     base,
     grad_new,
     edges_t,
     scatter,
     halo_hot,
-    w1,
-    w2,
-    nodes,
-    edges,
-    d_new,
-    d_agg,
-    senders,
-    receivers,
-    sems,
 ):
-    pairs = (
-        (senders_hbm, senders),
-        (receivers_hbm, receivers),
-        (nodes_hbm, nodes),
-        (w1_hbm, w1),
-        (edges_hbm, edges),
-        (d_agg_hbm, d_agg),
-        (d_new_hbm, d_new),
-        (w2_hbm, w2),
-    )
-    copies = [pltpu.make_async_copy(a, b, sems.at[i]) for i, (a, b) in enumerate(pairs)]
-    for copy in copies:
-        copy.start()
     here = lax.axis_index("patch")
     odd = here % 2
-    copies[0].wait()
-    copies[1].wait()
     owner = senders[...] // (ROWS * 8)
     offset = senders[...] % ROWS
     lower = jnp.where(here == 0, 63, here - 1)
@@ -110,7 +108,7 @@
     def columns(index, part):
         return jnp.broadcast_to(index[part : part + 1, :], (128, 128)).T
 
-    lane = lax.broadcasted_iota(jnp.int32, (128, 128), 1)
+    lane = lane_ref[...]
     send_hot, recv_hot = [], []
     for part in range(SLOTS // 128):
         place = columns(position, part)
@@ -124,8 +122,6 @@
         scatter[ROWS + 2 * HALO :, row] = hot(
             lax.broadcasted_iota(jnp.int32, (128, 128), 0) == receive[part : part + 1, :]
         )
-    copies[2].wait()
-    copies[3].wait()
     product = jnp.concatenate(
         [
             halves(dot(nodes[...], w1[WIDTH : 2 * WIDTH])),
@@ -133,7 +129,6 @@
         ],
         axis=0,
     )
-    copies[4].wait()
     for start in range(0, SLOTS, BLOCK):
         rows = slice(start, start + BLOCK)
         parts = range(start // 128, (start + BLOCK) // 128)
@@ -146,8 +141,6 @@
         )
         base[rows, :] = dot(edges[rows, :], w1[:WIDTH]) + dot(gather, product)
         edges_t[:, rows] = edges[rows, :].T
-    copies[5].wait()
-    copies[6].wait()
     limit = jnp.broadcast_to(count[0:1, 0:1], (SLOTS, 1))
     for start in range(0, SLOTS, BLOCK):
         rows = slice(start, start + BLOCK)
@@ -156,7 +149,6 @@
         live = jnp.where(slot < limit[rows], 1.0, 0.0)
         taken = dot(jnp.concatenate([recv_hot[p] for p in parts], axis=0), d_agg[...])
         grad_new[rows, :] = live * (d_new[rows, :].astype(F32) + taken)
-    copies[7].wait()
 
 
 def prepare(*args):
@@ -166,25 +158,13 @@
         ((WIDTH, SLOTS), BF16),
         ((PLACES, SLOTS), BF16),
         ((SLOTS, 128), BF16),
-        ((3 * WIDTH, WIDTH), BF16),
-        ((WIDTH, WIDTH), BF16),
-        ((ROWS, WIDTH), BF16),
-    )
-    args = args[:1] + tuple(pltpu.with_memory_space_constraint(a, pltpu.HBM) for a in args[1:])
+    )
     return pl.pallas_call(
         prepare_kernel,
         out_shape=[pltpu.VMEM(s, d) for s, d in shapes],
-        in_specs=[VMEM] + [HBM] * 8,
-        out_specs=[VMEM] * 8,
-        scratch_shapes=[
-            pltpu.VMEM((SLOTS, WIDTH), BF16),
-            pltpu.VMEM((SLOTS, WIDTH), BF16),
-            pltpu.VMEM((ROWS, WIDTH), BF16),
-            pltpu.VMEM((6, 128), jnp.int32),
-            pltpu.VMEM((6, 128), jnp.int32),
-            pltpu.SemaphoreType.DMA((8,)),
-        ],
-        compiler_params=pltpu.CompilerParams(vmem_limit_bytes=20 * 1024 * 1024),
+        in_specs=[VMEM] * 9,
+        out_specs=[VMEM] * 5,
+        compiler_params=pltpu.CompilerParams(vmem_limit_bytes=16 * 1024 * 1024),
         cost_estimate=pl.CostEstimate(
             flops=2_000_000_000, bytes_accessed=10_000_000, transcendentals=0
         ),
@@ -210,9 +190,7 @@
     weight,
 ):
     odd = lax.axis_index("patch") % 2
-    first = pl.multiple_of(odd * (ROWS - HALO), HALO)
-    last = pl.multiple_of((1 - odd) * (ROWS - HALO), HALO)
-    halo = jnp.concatenate([pair[pl.ds(first, HALO), :], cross[pl.ds(last, HALO), :]], axis=0)
+    halo = jnp.concatenate([pair[...], cross[...]], axis=0)
     halo_product = halves(dot(halo, w1[WIDTH : 2 * WIDTH]))
     for start in range(0, SLOTS, BLOCK):
         rows = slice(start, start + BLOCK)
@@ -249,7 +227,7 @@
                 first = ((quad * 2 + y) * 4 + x) * 48 + core * 24
                 rows = pl.ds(pl.multiple_of(first, 8), 24)
                 pieces.append(weight[rows, z * HALF : z * HALF + HALF])
-            place = ((x * 2 + y) * 2 + z) * 96
+            place = ((x * 2 + PAIR_ORDER.index(y)) * 2 + PAIR_ORDER.index(z)) * 96
             target[place : place + 96, :] = jnp.concatenate(pieces, axis=0).astype(BF16)
 
 
@@ -317,16 +295,17 @@
 
 def near_kernel(terms, result):
     values = jnp.sum(terms[...].astype(F32), axis=0)
-    for quad in range(4):
+    for place, quad in enumerate(QUAD_ORDER):
         piece = values[quad * 24 : quad * 24 + 24].astype(BF16)
         for z in range(8):
-            result[quad * 8 + z] = piece
+            result[place * 8 + z] = piece
 
 
 def far_kernel(terms, result):
     for half in range(2):
-        values = terms[half].astype(F32)
-        for place in range(2 + half, 32, 2):
+        places = [i for i in range(32) if Z_ORDER[i % 8] % 2 == half]
+        values = terms[places[0]].astype(F32)
+        for place in places[1:]:
             values = values + terms[place].astype(F32)
         result[:, half * HALF : half * HALF + HALF] = values
 
@@ -336,24 +315,29 @@
 ):
     here = lax.axis_index("patch")
     odd = here % 2
-    cross = lax.ppermute(nodes, "patch", CROSS)
-    pair = lax.ppermute(nodes, "patch", PAIR)
-    base, grad_new, edges_t, scatter, halo_hot, w1, w2, own = prepare(
+    odd = lax.axis_index("patch") % 2
+    first, last = nodes[:HALO], nodes[ROWS - HALO :]
+    to_cross = jnp.where(odd == 0, first, last)
+    to_pair = jnp.where(odd == 0, last, first)
+    lane, to_cross, to_pair = lax.optimization_barrier((lane_index(to_cross), to_cross, to_pair))
+    cross = lax.ppermute(to_cross, "patch", CROSS)
+    pair = lax.ppermute(to_pair, "patch", PAIR)
+    base, grad_new, edges_t, scatter, halo_hot = prepare(
         jnp.broadcast_to(edge_count, (8, 128)),
         senders.reshape(6, 128),
         receivers.reshape(6, 128),
+        lane,
         nodes,
         edges,
         d_new_edges,
         d_aggregate,
         edge_w1,
-        edge_w2,
     )
     mine, theirs, dz, summed, ret_cross = weight_terms(
-        cross, pair, base, grad_new, edges_t, scatter, halo_hot, w1, w2, own
+        cross, pair, base, grad_new, edges_t, scatter, halo_hot, edge_w1, edge_w2, nodes
     )
     other = lax.ppermute(theirs, "patch", PAIR)
-    edge_grad, node_grad = finish(grad_new, summed, dz, w1)
+    edge_grad, node_grad = finish(grad_new, summed, dz, edge_w1)
     other, node_grad = lax.optimization_barrier((other, node_grad))
     from_pair = jnp.concatenate([other[2 * SLOTS : -HALO], other[-HALO:]], axis=1).astype(F32)
     weight = small_call(add_kernel, (2 * SLOTS, HALF), BF16, mine, other)

time: 69.9 us -> 67 us (0.959)
  the two profiles are of different devices: /device:TPU:8 before, /device:TPU:16 now
where the time goes in v4:
time: 67 us; the launch traced here: 66.6 us
  starting transfers between devices  23.2 us (35%)
  blocking collectives  19.8 us (30%)
  waiting for transfers between devices  11.9 us (18%)
  Pallas kernels  8.53 us (13%)
  other arithmetic  1.54 us (2%)
  between operations  1.53 us (2%)
    all_to_all x1, blocking collectives, exchange(): return lax.all_to_all(block, AXES, 0, 0, axis_index_groups=groups)  19.8 us
    all_to_all x1, starting transfers between devices, exchange(): return lax.all_to_all(block, AXES, 0, 0, axis_index_groups=groups)  12.2 us
    ppermute x1, waiting for transfers between devices, per_device(): from_cross = lax.ppermute(ret_cross, 'patch', CROSS).astype(F32)  7.16 us
    all_to_all x1, waiting for transfers between devices, exchange(): return lax.all_to_all(block, AXES, 0, 0, axis_index_groups=groups)  4.58 us
    ppermute x1, starting transfers between devices, per_device(): cross = lax.ppermute(to_cross, 'patch', CROSS)  4.26 us
    pallas_call x1, Pallas kernels, weight_terms(): pl.pallas_call(weight_kernel, out_shape=[pltpu.VMEM(s, d) for s, d in sha...  3.51 us
    ppermute x1, starting transfers between devices, per_device(): other = lax.ppermute(theirs, 'patch', PAIR)  2.42 us
    ppermute x1, starting transfers between devices, per_device(): from_cross = lax.ppermute(ret_cross, 'patch', CROSS).astype(F32)  2.38 us
  transfers between devices with their start and end apart: 5, of which 3 were waited for; matrix products, arithmetic and copies ran while one was open for 1% of the time, Pallas kernels for 5%

profile of v4, /device:TPU:16, one launch (start us, length us, event | category | flops | bytes accessed | tf_op | source)
XLA Modules:
  0.0 66.6 jit_solution(12246369058293786288)
XLA Ops:
  0.6 0.8 %broadcast_select_fusion = (bf16[32,512]{1,0:T(8,128)(2,1)S(1)}, bf16[32,512]{1,0:T(8,128)(2,1)S(1)}) fusion(pred[]{:T(512)S(6)} %eq.10, bf16[128,512]{1,0:T(8,128)(2,1)} %nodes.3), kind=kLoop, calls=%fused_computation.5 | loop fusion | flops 32768 | bytes 131073 | tf_op jit(solution)/shard_map/jit(_where)/select_n | solution.py:321
  1.4 0.0 copy-start
  1.4 0.0 copy-start.1
  1.4 0.0 copy-start.2
  1.5 0.0 copy-start.3
  1.5 0.0 copy-start.5
  1.5 0.0 copy-start.6
  1.5 0.0 copy-start.7
  1.5 4.3 %collective-permute-start = (bf16[32,512]{1,0:T(8,128)(2,1)S(1)}, bf16[32,512]{1,0:T(8,128)(2,1)S(1)}, u32[]{:S(2)}, u32[]{:S(2)}) collective-permute-start(bf16[32,512]{1,0:T(8,128)(2,1)S(1)} %get-tuple-element.22.after), channel_id=1, source_target_pairs={{0,504},{8,16},{16,8},{24,32},{32,24},{40,48},{48,40},{56,64},{64,... | collective-permute-start | bytes 98312 | tf_op jit(solution)/shard_map/ppermute | solution.py:323
  5.8 1.9 %collective-permute-start.1 = (bf16[32,512]{1,0:T(8,128)(2,1)S(1)}, bf16[32,512]{1,0:T(8,128)(2,1)S(1)}, u32[]{:S(2)}, u32[]{:S(2)}) collective-permute-start(bf16[32,512]{1,0:T(8,128)(2,1)S(1)} %get-tuple-element.23), channel_id=1, source_target_pairs={{0,8},{8,0},{16,24},{24,16},{32,40},{40,32},{48,56},{56,48},{64,72... | collective-permute-start | bytes 98312 | tf_op jit(solution)/shard_map/ppermute | solution.py:324
  8.4 0.0 copy-done
  8.4 0.0 copy-done.1
  8.4 0.0 copy-done.2
  8.4 0.0 copy-done.3
  8.4 0.0 copy-done.5
  8.4 0.0 copy-done.6
  8.4 0.0 copy-done.7
  8.4 0.0 copy-start.4
  8.5 1.5 %shard_map.116 = (f32[768,512]{1,0:T(8,128)S(1)}, f32[768,512]{1,0:T(8,128)S(1)}, bf16[512,768]{1,0:T(8,128)(2,1)S(1)}, bf16[320,768]{1,0:T(8,128)(2,1)S(1)}, bf16[768,128]{1,0:T(8,128)(2,1)S(1)}) custom-call(s32[8,128]{1,0:T(8,128)S(1)} %broadcast_in_dim.8.count, s32[6,128]{1,0:T(8,128)S(1)} %bitcast.6, s32[6,128]{1,0:T(8,128)S(1)} %bitcast.7, ...), custom_call_target="tpu_custom_call" | custom-call | flops 2000000000 | bytes 10000000 | tf_op jit(solution)/shard_map/pallas_call | solution.py:162
  9.9 0.0 collective-permute-done.cross
  9.9 0.0 collective-permute-done.1.pair
  10.0 0.0 copy-done.4
  10.0 3.5 %shard_map.117 = (bf16[1536,256]{1,0:T(8,128)(2,1)S(1)}, bf16[1600,256]{1,0:T(8,128)(2,1)S(1)}, bf16[768,512]{1,0:T(8,128)(2,1)S(1)}, bf16[320,512]{1,0:T(8,128)(2,1)S(1)}, bf16[32,512]{1,0:T(8,128)(2,1)S(1)}) custom-call(bf16[32,512]{1,0:T(8,128)(2,1)S(1)} %collective-permute-done.cross, bf16[32,512]{1,0:T(8,128)(2,1)S(1)} %collective-permute-done.1.pair, ...), custom_call_target="tpu_custom_call" | custom-call | flops 2000000000 | bytes 10000000 | tf_op jit(solution)/shard_map/pallas_call | solution.py:242
  13.5 2.4 %collective-permute-start.2 = (bf16[1600,256]{1,0:T(8,128)(2,1)S(1)}, bf16[1600,256]{1,0:T(8,128)(2,1)S(1)}, u32[]{:S(2)}, u32[]{:S(2)}) collective-permute-start(bf16[1600,256]{1,0:T(8,128)(2,1)S(1)} %get-tuple-element.30), channel_id=1, source_target_pairs={{0,8},{8,0},{16,24},{24,16},{32,40},{40,32},{48,56},{56,48},{64,72... | collective-permute-start | bytes 2457608 | tf_op jit(solution)/shard_map/ppermute | solution.py:339
  15.9 1.8 %shard_map.118 = (bf16[768,512]{1,0:T(8,128)(2,1)}, f32[128,512]{1,0:T(8,128)S(1)}) custom-call(f32[768,512]{1,0:T(8,128)S(1)} %get-tuple-element.26.grad_new, bf16[320,512]{1,0:T(8,128)(2,1)S(1)} %get-tuple-element.31.summed, bf16[768,512]{1,0:T(8,128)(2,1)S(1)} %get-tuple-element.32.dz, bf16[1536,512]{1,0:T(8,128)(2,1)S(1)} %copy-done), custom_call_target="tpu_custom_call" | custom-call | flops 1000000000 | bytes 5000000 | tf_op jit(solution)/shard_map/pallas_call | solution.py:263
  17.7 0.1 collective-permute-done.2.other
  17.8 0.2 shard_map.119
  18.0 19.8 %all_to_all.10.terms = bf16[16,96,256]{2,1,0:T(8,128)(2,1)S(1)} all-to-all(bf16[16,96,256]{2,1,0:T(8,128)(2,1)S(1)} %bitcast.5), channel_id=1, replica_groups={{65,64,1,0,81,80,17,16,97,96,33,32,113,112,49,48},{73,72,9,8,89,88,25,2..., dimensions={0} | all-to-all | bytes 1572864 | tf_op jit(solution)/shard_map/all_to_all | solution.py:279
  37.9 0.9 %shard_map.120 = bf16[32,24,256]{2,1,0:T(8,128)(2,1)} custom-call(bf16[16,96,256]{2,1,0:T(8,128)(2,1)S(1)} %all_to_all.10.terms), custom_call_target="tpu_custom_call" | custom-call | tf_op jit(solution)/shard_map/pallas_call | solution.py:283
  38.7 12.2 %all-to-all-start.1 = ((bf16[32,24,256]{2,1,0:T(8,128)(2,1)}), bf16[32,24,256]{2,1,0:T(8,128)(2,1)S(1)}, u32[]{:S(2)}, u32[]{:S(2)}) async-start(bf16[32,24,256]{2,1,0:T(8,128)(2,1)} %shard_map.120), calls=%async_computation.1 | async-start | bytes 786432 | tf_op jit(solution)/shard_map/all_to_all | solution.py:279
  51.0 0.1 pad.1.clone
  51.1 2.4 %collective-permute-start.3 = (bf16[32,512]{1,0:T(8,128)(2,1)S(1)}, bf16[32,512]{1,0:T(8,128)(2,1)S(1)}, u32[]{:S(2)}, u32[]{:S(2)}) collective-permute-start(bf16[32,512]{1,0:T(8,128)(2,1)S(1)} %get-tuple-element.38), channel_id=1, source_target_pairs={{0,504},{8,16},{16,8},{24,32},{32,24},{40,48},{48,40},{56,64},{64,... | collective-permute-start | bytes 98312 | tf_op jit(solution)/shard_map/ppermute | solution.py:347
  53.5 7.2 %collective-permute-done.3 = bf16[32,512]{1,0:T(8,128)(2,1)S(1)} collective-permute-done((bf16[32,512]{1,0:T(8,128)(2,1)S(1)}, bf16[32,512]{1,0:T(8,128)(2,1)S(1)}, u32[]{:S(2)}, u32[]{:S(2)}) %collective-permute-start.3) | collective-permute-done | bytes 32800 | tf_op jit(solution)/shard_map/ppermute | solution.py:347
  60.6 0.7 %fusion = bf16[128,512]{1,0:T(8,128)(2,1)} fusion(f32[128,512]{1,0:T(8,128)S(1)} %get-tuple-element.34, f32[32,512]{1,0:T(8,128)S(1)} %get-tuple-element.46, f32[32,512]{1,0:T(8,128)S(1)} %get-tuple-element.45, f32[128]{0:T(128)S(1)} %pad.1.clone), kind=kLoop, calls=%fused_computation.1 | loop fusion | flops 262144 | bytes 524800 | tf_op jit(solution)/shard_map/convert_element_type | solution.py:353
  61.4 4.6 %all-to-all-done.1.terms = bf16[32,24,256]{2,1,0:T(8,128)(2,1)S(1)} async-done(((bf16[32,24,256]{2,1,0:T(8,128)(2,1)}), bf16[32,24,256]{2,1,0:T(8,128)(2,1)S(1)}, u32[]{:S(2)}, u32[]{:S(2)}) %all-to-all-start.1) | async-done | bytes 393248 | tf_op jit(solution)/shard_map/all_to_all | solution.py:279
  66.0 0.7 %shard_map.121 = f32[24,512]{1,0:T(8,128)} custom-call(bf16[32,24,256]{2,1,0:T(8,128)(2,1)S(1)} %all-to-all-done.1.terms), custom_call_target="tpu_custom_call" | custom-call | tf_op jit(solution)/shard_map/pallas_call | solution.py:283
  (5 shorter events, 0.0 us)
Async XLA Ops:
  1.4 6.9 %copy-start = (bf16[1536,512]{1,0:T(8,128)(2,1)S(1)}, bf16[1536,512]{1,0:T(8,128)(2,1)}, u32[]{:S(2)}) copy-start(bf16[1536,512]{1,0:T(8,128)(2,1)} %w1.5) | copy-start | bytes 4718596
  1.4 6.9 %copy-start.1 = (bf16[128,512]{1,0:T(8,128)(2,1)S(1)}, bf16[128,512]{1,0:T(8,128)(2,1)}, u32[]{:S(2)}) copy-start(bf16[128,512]{1,0:T(8,128)(2,1)} %nodes.3) | copy-start | bytes 393220
  1.4 6.9 %copy-start.2 = (bf16[768,512]{1,0:T(8,128)(2,1)S(1)}, bf16[768,512]{1,0:T(8,128)(2,1)}, u32[]{:S(2)}) copy-start(bf16[768,512]{1,0:T(8,128)(2,1)} %edges.1) | copy-start | bytes 2359300
  1.5 6.9 %copy-start.3 = (bf16[768,512]{1,0:T(8,128)(2,1)S(1)}, bf16[768,512]{1,0:T(8,128)(2,1)}, u32[]{:S(2)}) copy-start(bf16[768,512]{1,0:T(8,128)(2,1)} %d_new.1) | copy-start | bytes 2359300
  1.5 6.9 %copy-start.5 = (bf16[128,512]{1,0:T(8,128)(2,1)S(1)}, bf16[128,512]{1,0:T(8,128)(2,1)}, u32[]{:S(2)}) copy-start(bf16[128,512]{1,0:T(8,128)(2,1)} %d_agg.1) | copy-start | bytes 393220
  1.5 6.9 %copy-start.6 = (s32[768]{0:T(1024)S(1)}, s32[768]{0:T(1024)}, u32[]{:S(2)}) copy-start(s32[768]{0:T(1024)} %param.15) | copy-start | bytes 9220
  1.5 6.9 %copy-start.7 = (s32[768]{0:T(1024)S(1)}, s32[768]{0:T(1024)}, u32[]{:S(2)}) copy-start(s32[768]{0:T(1024)} %param.16) | copy-start | bytes 9220
  1.5 8.4 %collective-permute-start = (bf16[32,512]{1,0:T(8,128)(2,1)S(1)}, bf16[32,512]{1,0:T(8,128)(2,1)S(1)}, u32[]{:S(2)}, u32[]{:S(2)}) collective-permute-start(bf16[32,512]{1,0:T(8,128)(2,1)S(1)} %get-tuple-element.22.after), channel_id=1, source_target_pairs={{0,504},{8,16},{16,8},{24,32},{32,24},{40,48},{48,40},{56,64},{64,... | collective-permute-start | bytes 98312 | tf_op jit(solution)/shard_map/ppermute | solution.py:323
  5.8 4.2 %collective-permute-start.1 = (bf16[32,512]{1,0:T(8,128)(2,1)S(1)}, bf16[32,512]{1,0:T(8,128)(2,1)S(1)}, u32[]{:S(2)}, u32[]{:S(2)}) collective-permute-start(bf16[32,512]{1,0:T(8,128)(2,1)S(1)} %get-tuple-element.23), channel_id=1, source_target_pairs={{0,8},{8,0},{16,24},{24,16},{32,40},{40,32},{48,56},{56,48},{64,72... | collective-permute-start | bytes 98312 | tf_op jit(solution)/shard_map/ppermute | solution.py:324
  8.4 1.5 %copy-start.4 = (bf16[512,512]{1,0:T(8,128)(2,1)S(1)}, bf16[512,512]{1,0:T(8,128)(2,1)}, u32[]{:S(2)}) copy-start(bf16[512,512]{1,0:T(8,128)(2,1)} %w2.1) | copy-start | bytes 1572868
  13.5 4.4 %collective-permute-start.2 = (bf16[1600,256]{1,0:T(8,128)(2,1)S(1)}, bf16[1600,256]{1,0:T(8,128)(2,1)S(1)}, u32[]{:S(2)}, u32[]{:S(2)}) collective-permute-start(bf16[1600,256]{1,0:T(8,128)(2,1)S(1)} %get-tuple-element.30), channel_id=1, source_target_pairs={{0,8},{8,0},{16,24},{24,16},{32,40},{40,32},{48,56},{56,48},{64,72... | collective-permute-start | bytes 2457608 | tf_op jit(solution)/shard_map/ppermute | solution.py:339
  38.7 27.2 %all-to-all-start.1 = ((bf16[32,24,256]{2,1,0:T(8,128)(2,1)}), bf16[32,24,256]{2,1,0:T(8,128)(2,1)S(1)}, u32[]{:S(2)}, u32[]{:S(2)}) async-start(bf16[32,24,256]{2,1,0:T(8,128)(2,1)} %shard_map.120), calls=%async_computation.1 | async-start | bytes 786432 | tf_op jit(solution)/shard_map/all_to_all | solution.py:279
  51.1 9.6 %collective-permute-start.3 = (bf16[32,512]{1,0:T(8,128)(2,1)S(1)}, bf16[32,512]{1,0:T(8,128)(2,1)S(1)}, u32[]{:S(2)}, u32[]{:S(2)}) collective-permute-start(bf16[32,512]{1,0:T(8,128)(2,1)S(1)} %get-tuple-element.38), channel_id=1, source_target_pairs={{0,504},{8,16},{16,8},{24,32},{32,24},{40,48},{48,40},{56,64},{64,... | collective-permute-start | bytes 98312 | tf_op jit(solution)/shard_map/ppermute | solution.py:347

commit v5 on v4

--- a/solution.py
+++ b/solution.py
@@ -31,11 +31,12 @@
     return groups
 
 
-PAIR_ORDER = (1, 0)
-QUAD_ORDER = (1, 2, 3, 0)
-Z_ORDER = (7, 6, 5, 4, 3, 2, 1, 0)
-PAIRS_OF_8 = [[2 * i + k for k in PAIR_ORDER] for i in range(4)]
-NEAR = device_groups(PAIRS_OF_8, [list(range(4))], PAIRS_OF_8)
+Y_ORDER = (0,1)
+ZP_ORDER = (1,0)
+X_ORDER = (2,3,0,1)
+QUAD_ORDER = (1,2,3,0)
+Z_ORDER = (7,6,5,4,3,2,1,0)
+NEAR = device_groups([[2 * i + k for k in Y_ORDER] for i in range(4)], [X_ORDER], [[2 * i + k for k in ZP_ORDER] for i in range(4)])
 FAR = device_groups(
     [[2 * q + k for q in QUAD_ORDER] for k in range(2)], [[i] for i in range(4)], [Z_ORDER]
 )
@@ -227,7 +228,7 @@
                 first = ((quad * 2 + y) * 4 + x) * 48 + core * 24
                 rows = pl.ds(pl.multiple_of(first, 8), 24)
                 pieces.append(weight[rows, z * HALF : z * HALF + HALF])
-            place = ((x * 2 + PAIR_ORDER.index(y)) * 2 + PAIR_ORDER.index(z)) * 96
+            place = ((X_ORDER.index(x) * 2 + Y_ORDER.index(y)) * 2 + ZP_ORDER.index(z)) * 96
             target[place : place + 96, :] = jnp.concatenate(pieces, axis=0).astype(BF16)
 
 

time: 67 us -> 67.1 us (level)
  the two profiles are of different devices: /device:TPU:16 before, /device:TPU:8 now
where the time goes in v5:
time: 67.1 us; the launch traced here: 66.7 us
  starting transfers between devices  23.5 us (35%)
  blocking collectives  20.7 us (31%)
  waiting for transfers between devices  10.7 us (16%)
  Pallas kernels  8.54 us (13%)
  other arithmetic  1.54 us (2%)
  between operations  1.53 us (2%)
    all_to_all x1, blocking collectives, exchange(): return lax.all_to_all(block, AXES, 0, 0, axis_index_groups=groups)  20.7 us
    all_to_all x1, starting transfers between devices, exchange(): return lax.all_to_all(block, AXES, 0, 0, axis_index_groups=groups)  12.2 us
    ppermute x1, waiting for transfers between devices, per_device(): from_cross = lax.ppermute(ret_cross, 'patch', CROSS).astype(F32)  5.58 us
    all_to_all x1, waiting for transfers between devices, exchange(): return lax.all_to_all(block, AXES, 0, 0, axis_index_groups=groups)  4.99 us
    ppermute x1, starting transfers between devices, per_device(): cross = lax.ppermute(to_cross, 'patch', CROSS)  4.26 us
    pallas_call x1, Pallas kernels, weight_terms(): pl.pallas_call(weight_kernel, out_shape=[pltpu.VMEM(s, d) for s, d in sha...  3.52 us
    ppermute x1, starting transfers between devices, per_device(): from_cross = lax.ppermute(ret_cross, 'patch', CROSS).astype(F32)  2.72 us
    ppermute x1, starting transfers between devices, per_device(): other = lax.ppermute(theirs, 'patch', PAIR)  2.4 us
  transfers between devices with their start and end apart: 5, of which 3 were waited for; matrix products, arithmetic and copies ran while one was open for 1% of the time, Pallas kernels for 5%

profile of v5, /device:TPU:8, one launch (start us, length us, event | category | flops | bytes accessed | tf_op | source)
XLA Modules:
  0.0 66.7 jit_solution(15815795851531755010)
XLA Ops:
  0.6 0.8 %broadcast_select_fusion = (bf16[32,512]{1,0:T(8,128)(2,1)S(1)}, bf16[32,512]{1,0:T(8,128)(2,1)S(1)}) fusion(pred[]{:T(512)S(6)} %eq.10, bf16[128,512]{1,0:T(8,128)(2,1)} %nodes.3), kind=kLoop, calls=%fused_computation.5 | loop fusion | flops 32768 | bytes 131073 | tf_op jit(solution)/shard_map/jit(_where)/select_n | solution.py:322
  1.4 0.0 copy-start
  1.4 0.0 copy-start.1
  1.4 0.0 copy-start.2
  1.5 0.0 copy-start.3
  1.5 0.0 copy-start.5
  1.5 0.0 copy-start.6
  1.5 0.0 copy-start.7
  1.5 4.3 %collective-permute-start = (bf16[32,512]{1,0:T(8,128)(2,1)S(1)}, bf16[32,512]{1,0:T(8,128)(2,1)S(1)}, u32[]{:S(2)}, u32[]{:S(2)}) collective-permute-start(bf16[32,512]{1,0:T(8,128)(2,1)S(1)} %get-tuple-element.22.after), channel_id=1, source_target_pairs={{0,504},{8,16},{16,8},{24,32},{32,24},{40,48},{48,40},{56,64},{64,... | collective-permute-start | bytes 98312 | tf_op jit(solution)/shard_map/ppermute | solution.py:324
  5.8 1.9 %collective-permute-start.1 = (bf16[32,512]{1,0:T(8,128)(2,1)S(1)}, bf16[32,512]{1,0:T(8,128)(2,1)S(1)}, u32[]{:S(2)}, u32[]{:S(2)}) collective-permute-start(bf16[32,512]{1,0:T(8,128)(2,1)S(1)} %get-tuple-element.23), channel_id=1, source_target_pairs={{0,8},{8,0},{16,24},{24,16},{32,40},{40,32},{48,56},{56,48},{64,72... | collective-permute-start | bytes 98312 | tf_op jit(solution)/shard_map/ppermute | solution.py:325
  8.4 0.0 copy-done
  8.4 0.0 copy-done.1
  8.4 0.0 copy-done.2
  8.4 0.0 copy-done.3
  8.4 0.0 copy-done.5
  8.4 0.0 copy-done.6
  8.4 0.0 copy-done.7
  8.4 0.0 copy-start.4
  8.5 1.5 %shard_map.116 = (f32[768,512]{1,0:T(8,128)S(1)}, f32[768,512]{1,0:T(8,128)S(1)}, bf16[512,768]{1,0:T(8,128)(2,1)S(1)}, bf16[320,768]{1,0:T(8,128)(2,1)S(1)}, bf16[768,128]{1,0:T(8,128)(2,1)S(1)}) custom-call(s32[8,128]{1,0:T(8,128)S(1)} %broadcast_in_dim.8.count, s32[6,128]{1,0:T(8,128)S(1)} %bitcast.6, s32[6,128]{1,0:T(8,128)S(1)} %bitcast.7, ...), custom_call_target="tpu_custom_call" | custom-call | flops 2000000000 | bytes 10000000 | tf_op jit(solution)/shard_map/pallas_call | solution.py:163
  9.9 0.0 collective-permute-done.cross
  9.9 0.0 collective-permute-done.1.pair
  10.0 0.0 copy-done.4
  10.0 3.5 %shard_map.117 = (bf16[1536,256]{1,0:T(8,128)(2,1)S(1)}, bf16[1600,256]{1,0:T(8,128)(2,1)S(1)}, bf16[768,512]{1,0:T(8,128)(2,1)S(1)}, bf16[320,512]{1,0:T(8,128)(2,1)S(1)}, bf16[32,512]{1,0:T(8,128)(2,1)S(1)}) custom-call(bf16[32,512]{1,0:T(8,128)(2,1)S(1)} %collective-permute-done.cross, bf16[32,512]{1,0:T(8,128)(2,1)S(1)} %collective-permute-done.1.pair, ...), custom_call_target="tpu_custom_call" | custom-call | flops 2000000000 | bytes 10000000 | tf_op jit(solution)/shard_map/pallas_call | solution.py:243
  13.5 2.4 %collective-permute-start.2 = (bf16[1600,256]{1,0:T(8,128)(2,1)S(1)}, bf16[1600,256]{1,0:T(8,128)(2,1)S(1)}, u32[]{:S(2)}, u32[]{:S(2)}) collective-permute-start(bf16[1600,256]{1,0:T(8,128)(2,1)S(1)} %get-tuple-element.30), channel_id=1, source_target_pairs={{0,8},{8,0},{16,24},{24,16},{32,40},{40,32},{48,56},{56,48},{64,72... | collective-permute-start | bytes 2457608 | tf_op jit(solution)/shard_map/ppermute | solution.py:340
  15.9 1.8 %shard_map.118 = (bf16[768,512]{1,0:T(8,128)(2,1)}, f32[128,512]{1,0:T(8,128)S(1)}) custom-call(f32[768,512]{1,0:T(8,128)S(1)} %get-tuple-element.26.grad_new, bf16[320,512]{1,0:T(8,128)(2,1)S(1)} %get-tuple-element.31.summed, bf16[768,512]{1,0:T(8,128)(2,1)S(1)} %get-tuple-element.32.dz, bf16[1536,512]{1,0:T(8,128)(2,1)S(1)} %copy-done), custom_call_target="tpu_custom_call" | custom-call | flops 1000000000 | bytes 5000000 | tf_op jit(solution)/shard_map/pallas_call | solution.py:264
  17.7 0.1 collective-permute-done.2.other
  17.8 0.2 shard_map.119
  18.0 20.7 %all_to_all.10.terms = bf16[16,96,256]{2,1,0:T(8,128)(2,1)S(1)} all-to-all(bf16[16,96,256]{2,1,0:T(8,128)(2,1)S(1)} %bitcast.5), channel_id=1, replica_groups={{33,32,97,96,49,48,113,112,1,0,65,64,17,16,81,80},{41,40,105,104,57,56,..., dimensions={0} | all-to-all | bytes 1572864 | tf_op jit(solution)/shard_map/all_to_all | solution.py:280
  38.7 0.9 %shard_map.120 = bf16[32,24,256]{2,1,0:T(8,128)(2,1)} custom-call(bf16[16,96,256]{2,1,0:T(8,128)(2,1)S(1)} %all_to_all.10.terms), custom_call_target="tpu_custom_call" | custom-call | tf_op jit(solution)/shard_map/pallas_call | solution.py:284
  39.6 12.2 %all-to-all-start.1 = ((bf16[32,24,256]{2,1,0:T(8,128)(2,1)}), bf16[32,24,256]{2,1,0:T(8,128)(2,1)S(1)}, u32[]{:S(2)}, u32[]{:S(2)}) async-start(bf16[32,24,256]{2,1,0:T(8,128)(2,1)} %shard_map.120), calls=%async_computation.1 | async-start | bytes 786432 | tf_op jit(solution)/shard_map/all_to_all | solution.py:280
  51.9 0.1 pad.1.clone
  51.9 2.7 %collective-permute-start.3 = (bf16[32,512]{1,0:T(8,128)(2,1)S(1)}, bf16[32,512]{1,0:T(8,128)(2,1)S(1)}, u32[]{:S(2)}, u32[]{:S(2)}) collective-permute-start(bf16[32,512]{1,0:T(8,128)(2,1)S(1)} %get-tuple-element.38), channel_id=1, source_target_pairs={{0,504},{8,16},{16,8},{24,32},{32,24},{40,48},{48,40},{56,64},{64,... | collective-permute-start | bytes 98312 | tf_op jit(solution)/shard_map/ppermute | solution.py:348
  54.7 5.6 %collective-permute-done.3 = bf16[32,512]{1,0:T(8,128)(2,1)S(1)} collective-permute-done((bf16[32,512]{1,0:T(8,128)(2,1)S(1)}, bf16[32,512]{1,0:T(8,128)(2,1)S(1)}, u32[]{:S(2)}, u32[]{:S(2)}) %collective-permute-start.3) | collective-permute-done | bytes 32800 | tf_op jit(solution)/shard_map/ppermute | solution.py:348
  60.3 0.7 %fusion = bf16[128,512]{1,0:T(8,128)(2,1)} fusion(f32[128,512]{1,0:T(8,128)S(1)} %get-tuple-element.34, f32[32,512]{1,0:T(8,128)S(1)} %get-tuple-element.46, f32[32,512]{1,0:T(8,128)S(1)} %get-tuple-element.45, f32[128]{0:T(128)S(1)} %pad.1.clone), kind=kLoop, calls=%fused_computation.1 | loop fusion | flops 262144 | bytes 524800 | tf_op jit(solution)/shard_map/convert_element_type | solution.py:354
  61.0 5.0 %all-to-all-done.1.terms = bf16[32,24,256]{2,1,0:T(8,128)(2,1)S(1)} async-done(((bf16[32,24,256]{2,1,0:T(8,128)(2,1)}), bf16[32,24,256]{2,1,0:T(8,128)(2,1)S(1)}, u32[]{:S(2)}, u32[]{:S(2)}) %all-to-all-start.1) | async-done | bytes 393248 | tf_op jit(solution)/shard_map/all_to_all | solution.py:280
  66.0 0.7 %shard_map.121 = f32[24,512]{1,0:T(8,128)} custom-call(bf16[32,24,256]{2,1,0:T(8,128)(2,1)S(1)} %all-to-all-done.1.terms), custom_call_target="tpu_custom_call" | custom-call | tf_op jit(solution)/shard_map/pallas_call | solution.py:284
  (5 shorter events, 0.0 us)
Async XLA Ops:
  1.4 6.9 %copy-start = (bf16[1536,512]{1,0:T(8,128)(2,1)S(1)}, bf16[1536,512]{1,0:T(8,128)(2,1)}, u32[]{:S(2)}) copy-start(bf16[1536,512]{1,0:T(8,128)(2,1)} %w1.5) | copy-start | bytes 4718596
  1.4 6.9 %copy-start.1 = (bf16[128,512]{1,0:T(8,128)(2,1)S(1)}, bf16[128,512]{1,0:T(8,128)(2,1)}, u32[]{:S(2)}) copy-start(bf16[128,512]{1,0:T(8,128)(2,1)} %nodes.3) | copy-start | bytes 393220
  1.4 6.9 %copy-start.2 = (bf16[768,512]{1,0:T(8,128)(2,1)S(1)}, bf16[768,512]{1,0:T(8,128)(2,1)}, u32[]{:S(2)}) copy-start(bf16[768,512]{1,0:T(8,128)(2,1)} %edges.1) | copy-start | bytes 2359300
  1.5 6.9 %copy-start.3 = (bf16[768,512]{1,0:T(8,128)(2,1)S(1)}, bf16[768,512]{1,0:T(8,128)(2,1)}, u32[]{:S(2)}) copy-start(bf16[768,512]{1,0:T(8,128)(2,1)} %d_new.1) | copy-start | bytes 2359300
  1.5 6.9 %copy-start.5 = (bf16[128,512]{1,0:T(8,128)(2,1)S(1)}, bf16[128,512]{1,0:T(8,128)(2,1)}, u32[]{:S(2)}) copy-start(bf16[128,512]{1,0:T(8,128)(2,1)} %d_agg.1) | copy-start | bytes 393220
  1.5 6.9 %copy-start.6 = (s32[768]{0:T(1024)S(1)}, s32[768]{0:T(1024)}, u32[]{:S(2)}) copy-start(s32[768]{0:T(1024)} %param.15) | copy-start | bytes 9220
  1.5 6.9 %copy-start.7 = (s32[768]{0:T(1024)S(1)}, s32[768]{0:T(1024)}, u32[]{:S(2)}) copy-start(s32[768]{0:T(1024)} %param.16) | copy-start | bytes 9220
  1.5 8.4 %collective-permute-start = (bf16[32,512]{1,0:T(8,128)(2,1)S(1)}, bf16[32,512]{1,0:T(8,128)(2,1)S(1)}, u32[]{:S(2)}, u32[]{:S(2)}) collective-permute-start(bf16[32,512]{1,0:T(8,128)(2,1)S(1)} %get-tuple-element.22.after), channel_id=1, source_target_pairs={{0,504},{8,16},{16,8},{24,32},{32,24},{40,48},{48,40},{56,64},{64,... | collective-permute-start | bytes 98312 | tf_op jit(solution)/shard_map/ppermute | solution.py:324
  5.8 4.2 %collective-permute-start.1 = (bf16[32,512]{1,0:T(8,128)(2,1)S(1)}, bf16[32,512]{1,0:T(8,128)(2,1)S(1)}, u32[]{:S(2)}, u32[]{:S(2)}) collective-permute-start(bf16[32,512]{1,0:T(8,128)(2,1)S(1)} %get-tuple-element.23), channel_id=1, source_target_pairs={{0,8},{8,0},{16,24},{24,16},{32,40},{40,32},{48,56},{56,48},{64,72... | collective-permute-start | bytes 98312 | tf_op jit(solution)/shard_map/ppermute | solution.py:325
  8.4 1.5 %copy-start.4 = (bf16[512,512]{1,0:T(8,128)(2,1)S(1)}, bf16[512,512]{1,0:T(8,128)(2,1)}, u32[]{:S(2)}) copy-start(bf16[512,512]{1,0:T(8,128)(2,1)} %w2.1) | copy-start | bytes 1572868
  13.5 4.3 %collective-permute-start.2 = (bf16[1600,256]{1,0:T(8,128)(2,1)S(1)}, bf16[1600,256]{1,0:T(8,128)(2,1)S(1)}, u32[]{:S(2)}, u32[]{:S(2)}) collective-permute-start(bf16[1600,256]{1,0:T(8,128)(2,1)S(1)} %get-tuple-element.30), channel_id=1, source_target_pairs={{0,8},{8,0},{16,24},{24,16},{32,40},{40,32},{48,56},{56,48},{64,72... | collective-permute-start | bytes 2457608 | tf_op jit(solution)/shard_map/ppermute | solution.py:340
  39.6 26.4 %all-to-all-start.1 = ((bf16[32,24,256]{2,1,0:T(8,128)(2,1)}), bf16[32,24,256]{2,1,0:T(8,128)(2,1)S(1)}, u32[]{:S(2)}, u32[]{:S(2)}) async-start(bf16[32,24,256]{2,1,0:T(8,128)(2,1)} %shard_map.120), calls=%async_computation.1 | async-start | bytes 786432 | tf_op jit(solution)/shard_map/all_to_all | solution.py:280
  51.9 8.3 %collective-permute-start.3 = (bf16[32,512]{1,0:T(8,128)(2,1)S(1)}, bf16[32,512]{1,0:T(8,128)(2,1)S(1)}, u32[]{:S(2)}, u32[]{:S(2)}) collective-permute-start(bf16[32,512]{1,0:T(8,128)(2,1)S(1)} %get-tuple-element.38), channel_id=1, source_target_pairs={{0,504},{8,16},{16,8},{24,32},{32,24},{40,48},{48,40},{56,64},{64,... | collective-permute-start | bytes 98312 | tf_op jit(solution)/shard_map/ppermute | solution.py:348

commit v6 on v5

--- a/solution.py
+++ b/solution.py
@@ -125,8 +125,8 @@
         )
     product = jnp.concatenate(
         [
-            halves(dot(nodes[...], w1[WIDTH : 2 * WIDTH])),
-            halves(dot(nodes[...], w1[2 * WIDTH :])),
+            dot(nodes[...], w1[WIDTH : 2 * WIDTH]).astype(BF16),
+            dot(nodes[...], w1[2 * WIDTH :]).astype(BF16),
         ],
         axis=0,
     )
@@ -135,7 +135,7 @@
         parts = range(start // 128, (start + BLOCK) // 128)
         gather = jnp.concatenate(
             [
-                jnp.concatenate([send_hot[p], send_hot[p], recv_hot[p], recv_hot[p]], axis=1)
+                jnp.concatenate([send_hot[p], recv_hot[p]], axis=1)
                 for p in parts
             ],
             axis=0,
@@ -302,20 +302,40 @@
             result[place * 8 + z] = piece
 
 
-def far_kernel(terms, result):
+def far_kernel(terms, node_grad, other, from_cross, weight_grad, d_nodes):
     for half in range(2):
         places = [i for i in range(32) if Z_ORDER[i % 8] % 2 == half]
         values = terms[places[0]].astype(F32)
         for place in places[1:]:
             values = values + terms[place].astype(F32)
-        result[:, half * HALF : half * HALF + HALF] = values
+        weight_grad[:, half * HALF : half * HALF + HALF] = values
+    odd = lax.axis_index("patch") % 2 == 1
+    left, right = other[2 * SLOTS : 2 * SLOTS + HALO], other[2 * SLOTS + HALO :]
+    from_pair = jnp.concatenate([left, right], axis=1).astype(F32)
+    across = from_cross[...].astype(F32)
+    lower = node_grad[:HALO] + jnp.where(odd, from_pair, across)
+    upper = node_grad[ROWS - HALO :] + jnp.where(odd, across, from_pair)
+    d_nodes[:HALO] = lower.astype(BF16)
+    d_nodes[HALO : ROWS - HALO] = node_grad[HALO : ROWS - HALO].astype(BF16)
+    d_nodes[ROWS - HALO :] = upper.astype(BF16)
+
+
+def last_sums(*args):
+    return pl.pallas_call(
+        far_kernel,
+        out_shape=[
+            jax.ShapeDtypeStruct((24, WIDTH), F32),
+            jax.ShapeDtypeStruct((ROWS, WIDTH), BF16),
+        ],
+        in_specs=[VMEM] * 4,
+        out_specs=[VMEM] * 2,
+        compiler_params=pltpu.CompilerParams(vmem_limit_bytes=8 * 1024 * 1024),
+    )(*args)
 
 
 def per_device(
     nodes, edges, d_new_edges, d_aggregate, edge_w1, edge_w2, senders, receivers, edge_count
 ):
-    here = lax.axis_index("patch")
-    odd = here % 2
     odd = lax.axis_index("patch") % 2
     first, last = nodes[:HALO], nodes[ROWS - HALO :]
     to_cross = jnp.where(odd == 0, first, last)
@@ -340,18 +360,13 @@
     other = lax.ppermute(theirs, "patch", PAIR)
     edge_grad, node_grad = finish(grad_new, summed, dz, edge_w1)
     other, node_grad = lax.optimization_barrier((other, node_grad))
-    from_pair = jnp.concatenate([other[2 * SLOTS : -HALO], other[-HALO:]], axis=1).astype(F32)
     weight = small_call(add_kernel, (2 * SLOTS, HALF), BF16, mine, other)
     weight = exchange(weight.reshape(16, 96, HALF), NEAR)
     weight = small_call(near_kernel, (32, 24, HALF), BF16, weight)
     weight, ret_cross = lax.optimization_barrier((weight, ret_cross))
-    from_cross = lax.ppermute(ret_cross, "patch", CROSS).astype(F32)
-    weight_grad = small_call(far_kernel, (24, WIDTH), F32, exchange(weight, FAR))
-    from_lower = jnp.where(odd == 1, from_pair, from_cross)
-    from_upper = jnp.where(odd == 1, from_cross, from_pair)
-    gap = jnp.zeros((ROWS - 2 * HALO, WIDTH), F32)
-    node_grad = node_grad + jnp.concatenate([from_lower, gap, from_upper], axis=0)
-    return (node_grad.astype(BF16), edge_grad, weight_grad)
+    from_cross = lax.ppermute(ret_cross, "patch", CROSS)
+    weight_grad, node_grad = last_sums(exchange(weight, FAR), node_grad, other, from_cross)
+    return (node_grad, edge_grad, weight_grad)
 
 
 def solution(mesh):

time: 67.1 us -> 67 us (level)
  waiting for transfers between devices: 10.7 us -> 11.5 us
  other arithmetic: 1.54 us -> 0.79 us
    all_to_all x1, waiting for transfers between devices: 4.99 us -> 5.75 us  [exchange(): return lax.all_to_all(block, AXES, 0, 0, axis_index_groups=groups)]
    convert_element_type x1 -> x0, other arithmetic: 0.74 us -> none  [per_device(): return (node_grad.astype(BF16), edge_grad, weight_grad)]
    pallas_call x0 -> x1, Pallas kernels: none -> 0.73 us  [last_sums(): pl.pallas_call(far_kernel, out_shape=[jax.ShapeDtypeStruct((24, WIDTH), F...]
    pallas_call x3 -> x2, Pallas kernels: 1.71 us -> 1.04 us  [small_call(): pl.pallas_call(body, out_shape=pltpu.VMEM(shape, dtype) if dtype == BF16...]
  transfers between devices with their start and end apart: 5 -> 5, of which waited for: 3 -> 3; matrix products, arithmetic and copies ran while one was open for 1% -> 0% of each run, Pallas kernels for 5% -> 5%
where the time goes in v6:
time: 67 us; the launch traced here: 66.6 us
  starting transfers between devices  23.4 us (35%)
  blocking collectives  20.9 us (31%)
  waiting for transfers between devices  11.5 us (17%)
  Pallas kernels  8.45 us (13%)
  between operations  1.5 us (2%)
  other arithmetic  0.79 us (1%)
    all_to_all x1, blocking collectives, exchange(): return lax.all_to_all(block, AXES, 0, 0, axis_index_groups=groups)  20.9 us
    all_to_all x1, starting transfers between devices, exchange(): return lax.all_to_all(block, AXES, 0, 0, axis_index_groups=groups)  12.1 us
    all_to_all x1, waiting for transfers between devices, exchange(): return lax.all_to_all(block, AXES, 0, 0, axis_index_groups=groups)  5.75 us
    ppermute x1, waiting for transfers between devices, per_device(): from_cross = lax.ppermute(ret_cross, 'patch', CROSS)  5.67 us
    ppermute x1, starting transfers between devices, per_device(): cross = lax.ppermute(to_cross, 'patch', CROSS)  4.26 us
    pallas_call x1, Pallas kernels, weight_terms(): pl.pallas_call(weight_kernel, out_shape=[pltpu.VMEM(s, d) for s, d in sha...  3.51 us
    ppermute x1, starting transfers between devices, per_device(): from_cross = lax.ppermute(ret_cross, 'patch', CROSS)  2.73 us
    ppermute x1, starting transfers between devices, per_device(): other = lax.ppermute(theirs, 'patch', PAIR)  2.42 us
  transfers between devices with their start and end apart: 5, of which 3 were waited for; matrix products, arithmetic and copies ran while one was open for 0% of the time, Pallas kernels for 5%

profile of v6, /device:TPU:8, one launch (start us, length us, event | category | flops | bytes accessed | tf_op | source)
XLA Modules:
  0.0 66.6 jit_solution(8913154947819693568)
XLA Ops:
  0.6 0.8 %broadcast_select_fusion = (bf16[32,512]{1,0:T(8,128)(2,1)S(1)}, bf16[32,512]{1,0:T(8,128)(2,1)S(1)}) fusion(pred[]{:T(512)S(6)} %eq.6, bf16[128,512]{1,0:T(8,128)(2,1)} %nodes.3), kind=kLoop, calls=%fused_computation | loop fusion | flops 32768 | bytes 131073 | tf_op jit(solution)/shard_map/jit(_where)/select_n | solution.py:342
  1.4 0.0 copy-start
  1.4 0.0 copy-start.1
  1.4 0.0 copy-start.2
  1.5 0.0 copy-start.3
  1.5 0.0 copy-start.5
  1.5 0.0 copy-start.6
  1.5 0.0 copy-start.7
  1.5 4.3 %collective-permute-start = (bf16[32,512]{1,0:T(8,128)(2,1)S(1)}, bf16[32,512]{1,0:T(8,128)(2,1)S(1)}, u32[]{:S(2)}, u32[]{:S(2)}) collective-permute-start(bf16[32,512]{1,0:T(8,128)(2,1)S(1)} %get-tuple-element.24.after), channel_id=1, source_target_pairs={{0,504},{8,16},{16,8},{24,32},{32,24},{40,48},{48,40},{56,64},{64,... | collective-permute-start | bytes 98312 | tf_op jit(solution)/shard_map/ppermute | solution.py:344
  5.8 1.9 %collective-permute-start.1 = (bf16[32,512]{1,0:T(8,128)(2,1)S(1)}, bf16[32,512]{1,0:T(8,128)(2,1)S(1)}, u32[]{:S(2)}, u32[]{:S(2)}) collective-permute-start(bf16[32,512]{1,0:T(8,128)(2,1)S(1)} %get-tuple-element.25), channel_id=1, source_target_pairs={{0,8},{8,0},{16,24},{24,16},{32,40},{40,32},{48,56},{56,48},{64,72... | collective-permute-start | bytes 98312 | tf_op jit(solution)/shard_map/ppermute | solution.py:345
  8.4 0.0 copy-done
  8.4 0.0 copy-done.1
  8.4 0.0 copy-done.2
  8.4 0.0 copy-done.3
  8.4 0.0 copy-done.5
  8.4 0.0 copy-done.6
  8.4 0.0 copy-done.7
  8.4 0.0 copy-start.4
  8.5 1.3 %shard_map.116 = (f32[768,512]{1,0:T(8,128)S(1)}, f32[768,512]{1,0:T(8,128)S(1)}, bf16[512,768]{1,0:T(8,128)(2,1)S(1)}, bf16[320,768]{1,0:T(8,128)(2,1)S(1)}, bf16[768,128]{1,0:T(8,128)(2,1)S(1)}) custom-call(s32[8,128]{1,0:T(8,128)S(1)} %broadcast_in_dim.2.count, s32[6,128]{1,0:T(8,128)S(1)} %bitcast.6, s32[6,128]{1,0:T(8,128)S(1)} %bitcast.7, ...), custom_call_target="tpu_custom_call" | custom-call | flops 2000000000 | bytes 10000000 | tf_op jit(solution)/shard_map/pallas_call | solution.py:163
  9.8 0.0 collective-permute-done.cross
  9.8 0.0 collective-permute-done.1.pair
  9.8 0.0 copy-done.4
  9.8 3.5 %shard_map.117 = (bf16[1536,256]{1,0:T(8,128)(2,1)S(1)}, bf16[1600,256]{1,0:T(8,128)(2,1)S(1)}, bf16[768,512]{1,0:T(8,128)(2,1)S(1)}, bf16[320,512]{1,0:T(8,128)(2,1)S(1)}, bf16[32,512]{1,0:T(8,128)(2,1)S(1)}) custom-call(bf16[32,512]{1,0:T(8,128)(2,1)S(1)} %collective-permute-done.cross, bf16[32,512]{1,0:T(8,128)(2,1)S(1)} %collective-permute-done.1.pair, ...), custom_call_target="tpu_custom_call" | custom-call | flops 2000000000 | bytes 10000000 | tf_op jit(solution)/shard_map/pallas_call | solution.py:243
  13.3 2.4 %collective-permute-start.2 = (bf16[1600,256]{1,0:T(8,128)(2,1)S(1)}, bf16[1600,256]{1,0:T(8,128)(2,1)S(1)}, u32[]{:S(2)}, u32[]{:S(2)}) collective-permute-start(bf16[1600,256]{1,0:T(8,128)(2,1)S(1)} %get-tuple-element.33), channel_id=1, source_target_pairs={{0,8},{8,0},{16,24},{24,16},{32,40},{40,32},{48,56},{56,48},{64,72... | collective-permute-start | bytes 2457608 | tf_op jit(solution)/shard_map/ppermute | solution.py:360
  15.8 1.8 %shard_map.118 = (bf16[768,512]{1,0:T(8,128)(2,1)}, f32[128,512]{1,0:T(8,128)S(1)}) custom-call(f32[768,512]{1,0:T(8,128)S(1)} %get-tuple-element.28.grad_new, bf16[320,512]{1,0:T(8,128)(2,1)S(1)} %get-tuple-element.34.summed, bf16[768,512]{1,0:T(8,128)(2,1)S(1)} %get-tuple-element.35.dz, bf16[1536,512]{1,0:T(8,128)(2,1)S(1)} %copy-done), custom_call_target="tpu_custom_call" | custom-call | flops 1000000000 | bytes 5000000 | tf_op jit(solution)/shard_map/pallas_call | solution.py:264
  17.6 0.1 collective-permute-done.2.other
  17.7 0.2 shard_map.119
  17.9 20.9 %all_to_all.10.terms = bf16[16,96,256]{2,1,0:T(8,128)(2,1)S(1)} all-to-all(bf16[16,96,256]{2,1,0:T(8,128)(2,1)S(1)} %bitcast.5), channel_id=1, replica_groups={{33,32,97,96,49,48,113,112,1,0,65,64,17,16,81,80},{41,40,105,104,57,56,..., dimensions={0} | all-to-all | bytes 1572864 | tf_op jit(solution)/shard_map/all_to_all | solution.py:280
  38.7 0.9 %shard_map.120 = bf16[32,24,256]{2,1,0:T(8,128)(2,1)} custom-call(bf16[16,96,256]{2,1,0:T(8,128)(2,1)S(1)} %all_to_all.10.terms), custom_call_target="tpu_custom_call" | custom-call | tf_op jit(solution)/shard_map/pallas_call | solution.py:284
  39.6 12.1 %all-to-all-start.1 = ((bf16[32,24,256]{2,1,0:T(8,128)(2,1)}), bf16[32,24,256]{2,1,0:T(8,128)(2,1)S(1)}, u32[]{:S(2)}, u32[]{:S(2)}) async-start(bf16[32,24,256]{2,1,0:T(8,128)(2,1)} %shard_map.120), calls=%async_computation.1 | async-start | bytes 786432 | tf_op jit(solution)/shard_map/all_to_all | solution.py:280
  51.7 2.7 %collective-permute-start.3 = (bf16[32,512]{1,0:T(8,128)(2,1)S(1)}, bf16[32,512]{1,0:T(8,128)(2,1)S(1)}, u32[]{:S(2)}, u32[]{:S(2)}) collective-permute-start(bf16[32,512]{1,0:T(8,128)(2,1)S(1)} %get-tuple-element.41), channel_id=1, source_target_pairs={{0,504},{8,16},{16,8},{24,32},{32,24},{40,48},{48,40},{56,64},{64,... | collective-permute-start | bytes 98312 | tf_op jit(solution)/shard_map/ppermute | solution.py:367
  54.5 5.7 %collective-permute-done.3.from_cross = bf16[32,512]{1,0:T(8,128)(2,1)S(1)} collective-permute-done((bf16[32,512]{1,0:T(8,128)(2,1)S(1)}, bf16[32,512]{1,0:T(8,128)(2,1)S(1)}, u32[]{:S(2)}, u32[]{:S(2)}) %collective-permute-start.3) | collective-permute-done | bytes 32800 | tf_op jit(solution)/shard_map/ppermute | solution.py:367
  60.1 5.7 %all-to-all-done.1.terms = bf16[32,24,256]{2,1,0:T(8,128)(2,1)S(1)} async-done(((bf16[32,24,256]{2,1,0:T(8,128)(2,1)}), bf16[32,24,256]{2,1,0:T(8,128)(2,1)S(1)}, u32[]{:S(2)}, u32[]{:S(2)}) %all-to-all-start.1) | async-done | bytes 393248 | tf_op jit(solution)/shard_map/all_to_all | solution.py:280
  65.9 0.7 %shard_map.121 = (f32[24,512]{1,0:T(8,128)}, bf16[128,512]{1,0:T(8,128)(2,1)}) custom-call(bf16[32,24,256]{2,1,0:T(8,128)(2,1)S(1)} %all-to-all-done.1.terms, f32[128,512]{1,0:T(8,128)S(1)} %get-tuple-element.40.node_grad, bf16[1600,256]{1,0:T(8,128)(2,1)S(1)} %collective-permute-done.2.other, bf16[32,512]{1,0:T(8,128)(2,1)S(1)} %collective-permute-done.3.from_cross), custom_call_target="tpu_custom_call" | custom-call | tf_op jit(solution)/shard_map/pallas_call | solution.py:324
  (2 shorter events, 0.0 us)
Async XLA Ops:
  1.4 6.9 %copy-start = (bf16[1536,512]{1,0:T(8,128)(2,1)S(1)}, bf16[1536,512]{1,0:T(8,128)(2,1)}, u32[]{:S(2)}) copy-start(bf16[1536,512]{1,0:T(8,128)(2,1)} %w1.5) | copy-start | bytes 4718596
  1.4 6.9 %copy-start.1 = (bf16[128,512]{1,0:T(8,128)(2,1)S(1)}, bf16[128,512]{1,0:T(8,128)(2,1)}, u32[]{:S(2)}) copy-start(bf16[128,512]{1,0:T(8,128)(2,1)} %nodes.3) | copy-start | bytes 393220
  1.4 6.9 %copy-start.2 = (bf16[768,512]{1,0:T(8,128)(2,1)S(1)}, bf16[768,512]{1,0:T(8,128)(2,1)}, u32[]{:S(2)}) copy-start(bf16[768,512]{1,0:T(8,128)(2,1)} %edges.1) | copy-start | bytes 2359300
  1.5 6.9 %copy-start.3 = (bf16[768,512]{1,0:T(8,128)(2,1)S(1)}, bf16[768,512]{1,0:T(8,128)(2,1)}, u32[]{:S(2)}) copy-start(bf16[768,512]{1,0:T(8,128)(2,1)} %d_new.1) | copy-start | bytes 2359300
  1.5 6.9 %copy-start.5 = (bf16[128,512]{1,0:T(8,128)(2,1)S(1)}, bf16[128,512]{1,0:T(8,128)(2,1)}, u32[]{:S(2)}) copy-start(bf16[128,512]{1,0:T(8,128)(2,1)} %d_agg.1) | copy-start | bytes 393220
  1.5 6.9 %copy-start.6 = (s32[768]{0:T(1024)S(1)}, s32[768]{0:T(1024)}, u32[]{:S(2)}) copy-start(s32[768]{0:T(1024)} %param.15) | copy-start | bytes 9220
  1.5 6.9 %copy-start.7 = (s32[768]{0:T(1024)S(1)}, s32[768]{0:T(1024)}, u32[]{:S(2)}) copy-start(s32[768]{0:T(1024)} %param.16) | copy-start | bytes 9220
  1.5 8.3 %collective-permute-start = (bf16[32,512]{1,0:T(8,128)(2,1)S(1)}, bf16[32,512]{1,0:T(8,128)(2,1)S(1)}, u32[]{:S(2)}, u32[]{:S(2)}) collective-permute-start(bf16[32,512]{1,0:T(8,128)(2,1)S(1)} %get-tuple-element.24.after), channel_id=1, source_target_pairs={{0,504},{8,16},{16,8},{24,32},{32,24},{40,48},{48,40},{56,64},{64,... | collective-permute-start | bytes 98312 | tf_op jit(solution)/shard_map/ppermute | solution.py:344
  5.8 4.0 %collective-permute-start.1 = (bf16[32,512]{1,0:T(8,128)(2,1)S(1)}, bf16[32,512]{1,0:T(8,128)(2,1)S(1)}, u32[]{:S(2)}, u32[]{:S(2)}) collective-permute-start(bf16[32,512]{1,0:T(8,128)(2,1)S(1)} %get-tuple-element.25), channel_id=1, source_target_pairs={{0,8},{8,0},{16,24},{24,16},{32,40},{40,32},{48,56},{56,48},{64,72... | collective-permute-start | bytes 98312 | tf_op jit(solution)/shard_map/ppermute | solution.py:345
  8.4 1.4 %copy-start.4 = (bf16[512,512]{1,0:T(8,128)(2,1)S(1)}, bf16[512,512]{1,0:T(8,128)(2,1)}, u32[]{:S(2)}) copy-start(bf16[512,512]{1,0:T(8,128)(2,1)} %w2.1) | copy-start | bytes 1572868
  13.3 4.4 %collective-permute-start.2 = (bf16[1600,256]{1,0:T(8,128)(2,1)S(1)}, bf16[1600,256]{1,0:T(8,128)(2,1)S(1)}, u32[]{:S(2)}, u32[]{:S(2)}) collective-permute-start(bf16[1600,256]{1,0:T(8,128)(2,1)S(1)} %get-tuple-element.33), channel_id=1, source_target_pairs={{0,8},{8,0},{16,24},{24,16},{32,40},{40,32},{48,56},{56,48},{64,72... | collective-permute-start | bytes 2457608 | tf_op jit(solution)/shard_map/ppermute | solution.py:360
  39.6 26.3 %all-to-all-start.1 = ((bf16[32,24,256]{2,1,0:T(8,128)(2,1)}), bf16[32,24,256]{2,1,0:T(8,128)(2,1)S(1)}, u32[]{:S(2)}, u32[]{:S(2)}) async-start(bf16[32,24,256]{2,1,0:T(8,128)(2,1)} %shard_map.120), calls=%async_computation.1 | async-start | bytes 786432 | tf_op jit(solution)/shard_map/all_to_all | solution.py:280
  51.7 8.4 %collective-permute-start.3 = (bf16[32,512]{1,0:T(8,128)(2,1)S(1)}, bf16[32,512]{1,0:T(8,128)(2,1)S(1)}, u32[]{:S(2)}, u32[]{:S(2)}) collective-permute-start(bf16[32,512]{1,0:T(8,128)(2,1)S(1)} %get-tuple-element.41), channel_id=1, source_target_pairs={{0,504},{8,16},{16,8},{24,32},{32,24},{40,48},{48,40},{56,64},{64,... | collective-permute-start | bytes 98312 | tf_op jit(solution)/shard_map/ppermute | solution.py:367

commit v7 on v6

--- a/solution.py
+++ b/solution.py
@@ -125,8 +125,8 @@
         )
     product = jnp.concatenate(
         [
-            dot(nodes[...], w1[WIDTH : 2 * WIDTH]).astype(BF16),
-            dot(nodes[...], w1[2 * WIDTH :]).astype(BF16),
+            halves(dot(nodes[...], w1[WIDTH : 2 * WIDTH])),
+            halves(dot(nodes[...], w1[2 * WIDTH :])),
         ],
         axis=0,
     )
@@ -135,7 +135,7 @@
         parts = range(start // 128, (start + BLOCK) // 128)
         gather = jnp.concatenate(
             [
-                jnp.concatenate([send_hot[p], recv_hot[p]], axis=1)
+                jnp.concatenate([send_hot[p], send_hot[p], recv_hot[p], recv_hot[p]], axis=1)
                 for p in parts
             ],
             axis=0,

time: 67 us -> 67.1 us (level)
  no operation moved by 1% of the time
where the time goes in v7:
time: 67.1 us; the launch traced here: 66.7 us
  starting transfers between devices  23.6 us (35%)
  blocking collectives  20.7 us (31%)
  waiting for transfers between devices  11.5 us (17%)
  Pallas kernels  8.59 us (13%)
  between operations  1.5 us (2%)
  other arithmetic  0.79 us (1%)
    all_to_all x1, blocking collectives, exchange(): return lax.all_to_all(block, AXES, 0, 0, axis_index_groups=groups)  20.7 us
    all_to_all x1, starting transfers between devices, exchange(): return lax.all_to_all(block, AXES, 0, 0, axis_index_groups=groups)  12.2 us
    all_to_all x1, waiting for transfers between devices, exchange(): return lax.all_to_all(block, AXES, 0, 0, axis_index_groups=groups)  5.75 us
    ppermute x1, waiting for transfers between devices, per_device(): from_cross = lax.ppermute(ret_cross, 'patch', CROSS)  5.67 us
    ppermute x1, starting transfers between devices, per_device(): cross = lax.ppermute(to_cross, 'patch', CROSS)  4.26 us
    pallas_call x1, Pallas kernels, weight_terms(): pl.pallas_call(weight_kernel, out_shape=[pltpu.VMEM(s, d) for s, d in sha...  3.51 us
    ppermute x1, starting transfers between devices, per_device(): from_cross = lax.ppermute(ret_cross, 'patch', CROSS)  2.73 us
    ppermute x1, starting transfers between devices, per_device(): other = lax.ppermute(theirs, 'patch', PAIR)  2.42 us
  transfers between devices with their start and end apart: 5, of which 3 were waited for; matrix products, arithmetic and copies ran while one was open for 0% of the time, Pallas kernels for 5%

profile of v7, /device:TPU:8, one launch (start us, length us, event | category | flops | bytes accessed | tf_op | source)
XLA Modules:
  0.0 66.7 jit_solution(15835384463939700887)
XLA Ops:
  0.6 0.8 %broadcast_select_fusion = (bf16[32,512]{1,0:T(8,128)(2,1)S(1)}, bf16[32,512]{1,0:T(8,128)(2,1)S(1)}) fusion(pred[]{:T(512)S(6)} %eq.6, bf16[128,512]{1,0:T(8,128)(2,1)} %nodes.3), kind=kLoop, calls=%fused_computation | loop fusion | flops 32768 | bytes 131073 | tf_op jit(solution)/shard_map/jit(_where)/select_n | solution.py:342
  1.4 0.0 copy-start
  1.4 0.0 copy-start.1
  1.4 0.0 copy-start.2
  1.5 0.0 copy-start.3
  1.5 0.0 copy-start.5
  1.5 0.0 copy-start.6
  1.5 0.0 copy-start.7
  1.5 4.3 %collective-permute-start = (bf16[32,512]{1,0:T(8,128)(2,1)S(1)}, bf16[32,512]{1,0:T(8,128)(2,1)S(1)}, u32[]{:S(2)}, u32[]{:S(2)}) collective-permute-start(bf16[32,512]{1,0:T(8,128)(2,1)S(1)} %get-tuple-element.24.after), channel_id=1, source_target_pairs={{0,504},{8,16},{16,8},{24,32},{32,24},{40,48},{48,40},{56,64},{64,... | collective-permute-start | bytes 98312 | tf_op jit(solution)/shard_map/ppermute | solution.py:344
  5.8 1.9 %collective-permute-start.1 = (bf16[32,512]{1,0:T(8,128)(2,1)S(1)}, bf16[32,512]{1,0:T(8,128)(2,1)S(1)}, u32[]{:S(2)}, u32[]{:S(2)}) collective-permute-start(bf16[32,512]{1,0:T(8,128)(2,1)S(1)} %get-tuple-element.25), channel_id=1, source_target_pairs={{0,8},{8,0},{16,24},{24,16},{32,40},{40,32},{48,56},{56,48},{64,72... | collective-permute-start | bytes 98312 | tf_op jit(solution)/shard_map/ppermute | solution.py:345
  8.4 0.0 copy-done
  8.4 0.0 copy-done.1
  8.4 0.0 copy-done.2
  8.4 0.0 copy-done.3
  8.4 0.0 copy-done.5
  8.4 0.0 copy-done.6
  8.4 0.0 copy-done.7
  8.4 0.0 copy-start.4
  8.5 1.5 %shard_map.116 = (f32[768,512]{1,0:T(8,128)S(1)}, f32[768,512]{1,0:T(8,128)S(1)}, bf16[512,768]{1,0:T(8,128)(2,1)S(1)}, bf16[320,768]{1,0:T(8,128)(2,1)S(1)}, bf16[768,128]{1,0:T(8,128)(2,1)S(1)}) custom-call(s32[8,128]{1,0:T(8,128)S(1)} %broadcast_in_dim.2.count, s32[6,128]{1,0:T(8,128)S(1)} %bitcast.6, s32[6,128]{1,0:T(8,128)S(1)} %bitcast.7, ...), custom_call_target="tpu_custom_call" | custom-call | flops 2000000000 | bytes 10000000 | tf_op jit(solution)/shard_map/pallas_call | solution.py:163
  9.9 0.0 collective-permute-done.cross
  9.9 0.0 collective-permute-done.1.pair
  9.9 0.0 copy-done.4
  10.0 3.5 %shard_map.117 = (bf16[1536,256]{1,0:T(8,128)(2,1)S(1)}, bf16[1600,256]{1,0:T(8,128)(2,1)S(1)}, bf16[768,512]{1,0:T(8,128)(2,1)S(1)}, bf16[320,512]{1,0:T(8,128)(2,1)S(1)}, bf16[32,512]{1,0:T(8,128)(2,1)S(1)}) custom-call(bf16[32,512]{1,0:T(8,128)(2,1)S(1)} %collective-permute-done.cross, bf16[32,512]{1,0:T(8,128)(2,1)S(1)} %collective-permute-done.1.pair, ...), custom_call_target="tpu_custom_call" | custom-call | flops 2000000000 | bytes 10000000 | tf_op jit(solution)/shard_map/pallas_call | solution.py:243
  13.5 2.4 %collective-permute-start.2 = (bf16[1600,256]{1,0:T(8,128)(2,1)S(1)}, bf16[1600,256]{1,0:T(8,128)(2,1)S(1)}, u32[]{:S(2)}, u32[]{:S(2)}) collective-permute-start(bf16[1600,256]{1,0:T(8,128)(2,1)S(1)} %get-tuple-element.33), channel_id=1, source_target_pairs={{0,8},{8,0},{16,24},{24,16},{32,40},{40,32},{48,56},{56,48},{64,72... | collective-permute-start | bytes 2457608 | tf_op jit(solution)/shard_map/ppermute | solution.py:360
  15.9 1.8 %shard_map.118 = (bf16[768,512]{1,0:T(8,128)(2,1)}, f32[128,512]{1,0:T(8,128)S(1)}) custom-call(f32[768,512]{1,0:T(8,128)S(1)} %get-tuple-element.28.grad_new, bf16[320,512]{1,0:T(8,128)(2,1)S(1)} %get-tuple-element.34.summed, bf16[768,512]{1,0:T(8,128)(2,1)S(1)} %get-tuple-element.35.dz, bf16[1536,512]{1,0:T(8,128)(2,1)S(1)} %copy-done), custom_call_target="tpu_custom_call" | custom-call | flops 1000000000 | bytes 5000000 | tf_op jit(solution)/shard_map/pallas_call | solution.py:264
  17.7 0.1 collective-permute-done.2.other
  17.8 0.2 shard_map.119
  18.0 20.7 %all_to_all.10.terms = bf16[16,96,256]{2,1,0:T(8,128)(2,1)S(1)} all-to-all(bf16[16,96,256]{2,1,0:T(8,128)(2,1)S(1)} %bitcast.5), channel_id=1, replica_groups={{33,32,97,96,49,48,113,112,1,0,65,64,17,16,81,80},{41,40,105,104,57,56,..., dimensions={0} | all-to-all | bytes 1572864 | tf_op jit(solution)/shard_map/all_to_all | solution.py:280
  38.7 0.9 %shard_map.120 = bf16[32,24,256]{2,1,0:T(8,128)(2,1)} custom-call(bf16[16,96,256]{2,1,0:T(8,128)(2,1)S(1)} %all_to_all.10.terms), custom_call_target="tpu_custom_call" | custom-call | tf_op jit(solution)/shard_map/pallas_call | solution.py:284
  39.6 12.2 %all-to-all-start.1 = ((bf16[32,24,256]{2,1,0:T(8,128)(2,1)}), bf16[32,24,256]{2,1,0:T(8,128)(2,1)S(1)}, u32[]{:S(2)}, u32[]{:S(2)}) async-start(bf16[32,24,256]{2,1,0:T(8,128)(2,1)} %shard_map.120), calls=%async_computation.1 | async-start | bytes 786432 | tf_op jit(solution)/shard_map/all_to_all | solution.py:280
  51.9 2.7 %collective-permute-start.3 = (bf16[32,512]{1,0:T(8,128)(2,1)S(1)}, bf16[32,512]{1,0:T(8,128)(2,1)S(1)}, u32[]{:S(2)}, u32[]{:S(2)}) collective-permute-start(bf16[32,512]{1,0:T(8,128)(2,1)S(1)} %get-tuple-element.41), channel_id=1, source_target_pairs={{0,504},{8,16},{16,8},{24,32},{32,24},{40,48},{48,40},{56,64},{64,... | collective-permute-start | bytes 98312 | tf_op jit(solution)/shard_map/ppermute | solution.py:367
  54.6 5.7 %collective-permute-done.3.from_cross = bf16[32,512]{1,0:T(8,128)(2,1)S(1)} collective-permute-done((bf16[32,512]{1,0:T(8,128)(2,1)S(1)}, bf16[32,512]{1,0:T(8,128)(2,1)S(1)}, u32[]{:S(2)}, u32[]{:S(2)}) %collective-permute-start.3) | collective-permute-done | bytes 32800 | tf_op jit(solution)/shard_map/ppermute | solution.py:367
  60.3 5.7 %all-to-all-done.1.terms = bf16[32,24,256]{2,1,0:T(8,128)(2,1)S(1)} async-done(((bf16[32,24,256]{2,1,0:T(8,128)(2,1)}), bf16[32,24,256]{2,1,0:T(8,128)(2,1)S(1)}, u32[]{:S(2)}, u32[]{:S(2)}) %all-to-all-start.1) | async-done | bytes 393248 | tf_op jit(solution)/shard_map/all_to_all | solution.py:280
  66.0 0.7 %shard_map.121 = (f32[24,512]{1,0:T(8,128)}, bf16[128,512]{1,0:T(8,128)(2,1)}) custom-call(bf16[32,24,256]{2,1,0:T(8,128)(2,1)S(1)} %all-to-all-done.1.terms, f32[128,512]{1,0:T(8,128)S(1)} %get-tuple-element.40.node_grad, bf16[1600,256]{1,0:T(8,128)(2,1)S(1)} %collective-permute-done.2.other, bf16[32,512]{1,0:T(8,128)(2,1)S(1)} %collective-permute-done.3.from_cross), custom_call_target="tpu_custom_call" | custom-call | tf_op jit(solution)/shard_map/pallas_call | solution.py:324
  (2 shorter events, 0.0 us)
Async XLA Ops:
  1.4 6.9 %copy-start = (bf16[1536,512]{1,0:T(8,128)(2,1)S(1)}, bf16[1536,512]{1,0:T(8,128)(2,1)}, u32[]{:S(2)}) copy-start(bf16[1536,512]{1,0:T(8,128)(2,1)} %w1.5) | copy-start | bytes 4718596
  1.4 6.9 %copy-start.1 = (bf16[128,512]{1,0:T(8,128)(2,1)S(1)}, bf16[128,512]{1,0:T(8,128)(2,1)}, u32[]{:S(2)}) copy-start(bf16[128,512]{1,0:T(8,128)(2,1)} %nodes.3) | copy-start | bytes 393220
  1.4 6.9 %copy-start.2 = (bf16[768,512]{1,0:T(8,128)(2,1)S(1)}, bf16[768,512]{1,0:T(8,128)(2,1)}, u32[]{:S(2)}) copy-start(bf16[768,512]{1,0:T(8,128)(2,1)} %edges.1) | copy-start | bytes 2359300
  1.5 6.9 %copy-start.3 = (bf16[768,512]{1,0:T(8,128)(2,1)S(1)}, bf16[768,512]{1,0:T(8,128)(2,1)}, u32[]{:S(2)}) copy-start(bf16[768,512]{1,0:T(8,128)(2,1)} %d_new.1) | copy-start | bytes 2359300
  1.5 6.9 %copy-start.5 = (bf16[128,512]{1,0:T(8,128)(2,1)S(1)}, bf16[128,512]{1,0:T(8,128)(2,1)}, u32[]{:S(2)}) copy-start(bf16[128,512]{1,0:T(8,128)(2,1)} %d_agg.1) | copy-start | bytes 393220
  1.5 6.9 %copy-start.6 = (s32[768]{0:T(1024)S(1)}, s32[768]{0:T(1024)}, u32[]{:S(2)}) copy-start(s32[768]{0:T(1024)} %param.15) | copy-start | bytes 9220
  1.5 6.9 %copy-start.7 = (s32[768]{0:T(1024)S(1)}, s32[768]{0:T(1024)}, u32[]{:S(2)}) copy-start(s32[768]{0:T(1024)} %param.16) | copy-start | bytes 9220
  1.5 8.4 %collective-permute-start = (bf16[32,512]{1,0:T(8,128)(2,1)S(1)}, bf16[32,512]{1,0:T(8,128)(2,1)S(1)}, u32[]{:S(2)}, u32[]{:S(2)}) collective-permute-start(bf16[32,512]{1,0:T(8,128)(2,1)S(1)} %get-tuple-element.24.after), channel_id=1, source_target_pairs={{0,504},{8,16},{16,8},{24,32},{32,24},{40,48},{48,40},{56,64},{64,... | collective-permute-start | bytes 98312 | tf_op jit(solution)/shard_map/ppermute | solution.py:344
  5.8 4.2 %collective-permute-start.1 = (bf16[32,512]{1,0:T(8,128)(2,1)S(1)}, bf16[32,512]{1,0:T(8,128)(2,1)S(1)}, u32[]{:S(2)}, u32[]{:S(2)}) collective-permute-start(bf16[32,512]{1,0:T(8,128)(2,1)S(1)} %get-tuple-element.25), channel_id=1, source_target_pairs={{0,8},{8,0},{16,24},{24,16},{32,40},{40,32},{48,56},{56,48},{64,72... | collective-permute-start | bytes 98312 | tf_op jit(solution)/shard_map/ppermute | solution.py:345
  8.4 1.5 %copy-start.4 = (bf16[512,512]{1,0:T(8,128)(2,1)S(1)}, bf16[512,512]{1,0:T(8,128)(2,1)}, u32[]{:S(2)}) copy-start(bf16[512,512]{1,0:T(8,128)(2,1)} %w2.1) | copy-start | bytes 1572868
  13.5 4.4 %collective-permute-start.2 = (bf16[1600,256]{1,0:T(8,128)(2,1)S(1)}, bf16[1600,256]{1,0:T(8,128)(2,1)S(1)}, u32[]{:S(2)}, u32[]{:S(2)}) collective-permute-start(bf16[1600,256]{1,0:T(8,128)(2,1)S(1)} %get-tuple-element.33), channel_id=1, source_target_pairs={{0,8},{8,0},{16,24},{24,16},{32,40},{40,32},{48,56},{56,48},{64,72... | collective-permute-start | bytes 2457608 | tf_op jit(solution)/shard_map/ppermute | solution.py:360
  39.6 26.4 %all-to-all-start.1 = ((bf16[32,24,256]{2,1,0:T(8,128)(2,1)}), bf16[32,24,256]{2,1,0:T(8,128)(2,1)S(1)}, u32[]{:S(2)}, u32[]{:S(2)}) async-start(bf16[32,24,256]{2,1,0:T(8,128)(2,1)} %shard_map.120), calls=%async_computation.1 | async-start | bytes 786432 | tf_op jit(solution)/shard_map/all_to_all | solution.py:280
  51.9 8.4 %collective-permute-start.3 = (bf16[32,512]{1,0:T(8,128)(2,1)S(1)}, bf16[32,512]{1,0:T(8,128)(2,1)S(1)}, u32[]{:S(2)}, u32[]{:S(2)}) collective-permute-start(bf16[32,512]{1,0:T(8,128)(2,1)S(1)} %get-tuple-element.41), channel_id=1, source_target_pairs={{0,504},{8,16},{16,8},{24,32},{32,24},{40,48},{48,40},{56,64},{64,... | collective-permute-start | bytes 98312 | tf_op jit(solution)/shard_map/ppermute | solution.py:367
